TPU v7x, 32 devices: a whole 2x2x4 slice. The times are simulated.
32 devices in a mesh: section: 4 (over z), tensor: 2 (over x), dp: 4 (over y, core).
Axes of the slice: x: 2, y: 2, z: 4, core: 2. Of those that a mesh axis runs over, the one named last changes fastest.
Arguments:
- hidden_in: bfloat16 [8, 64, 4096], P('dp', None, 'tensor'), may hold values from -6 to 6
- lengths: int32 [8], P('dp'), may hold values from 16 to 64
- gains: bfloat16 [4, 4096], P('section', 'tensor'), may hold values from 0.25 to 1.75
- w_query: bfloat16 [4, 4096, 4096], P('section', None, 'tensor'), may hold values from -0.09375 to 0.09375
- w_keyval: bfloat16 [4, 4096, 8, 256], P('section', None, 'tensor'), may hold values from -0.09375 to 0.09375
- w_out: bfloat16 [4, 4096, 4096], P('section', 'tensor'), may hold values from -0.09375 to 0.09375
- grad_out: bfloat16 [8, 64, 4096], P('dp', None, 'tensor'), may hold values from -6 to 6
Outputs:
- grad_query: float32 [4, 4096, 4096], P('section', 'dp', 'tensor')
- grad_keyval: float32 [4, 4096, 8, 256], P('section', 'dp', 'tensor')
- grad_outproj: float32 [4, 4096, 4096], P('section', 'tensor', 'dp')
- grad_gain: float32 [4, 4096], P('section', ('tensor', 'dp'))
Inputs may be any that keep to these rules, and one draw needn't show every extreme that they name: `lengths`: A row's keys at positions at or beyond its length are padding.
All inputs are finite; a program needn't handle non-finite values.
Results may differ from a plain program's by a relative error of at most 0.035.
Values may be sent and summed in bfloat16 or wider, within the bound.
A program may use at most 256 MiB of HBM per device.

v0:
```python
import jax
import jax.numpy as jnp
from jax import lax
from jax.sharding import PartitionSpec as P

HEAD_DIM = 128


EPS = 1e-05
NEG = -1e30


def shifted(block, axis, distance):
    devices = range(lax.axis_size(axis))
    route = [(i - distance, i) for i in devices if i - distance in devices]
    return lax.ppermute(block, axis, route)


def features(operand):
    return lax.all_gather(operand, "tensor", axis=1, tiled=True)


def row_sum(operand):
    return lax.psum(operand, "tensor")


def head_total(operand):
    return lax.psum_scatter(operand, "tensor", scatter_dimension=1, tiled=True)


def neighbour(operand, offset):
    return shifted(operand, "section", offset)


def inner(former, latter):
    return lax.dot_general(
        former, latter, (((0,), (0,)), ((), ())), preferred_element_type=jnp.float32
    )


def outer_side(former, latter):
    return lax.dot_general(
        former, latter, (((1,), (1,)), ((), ())), preferred_element_type=jnp.float32
    )


def select_step(stacked, position):
    return lax.dynamic_index_in_dim(stacked, position, 0, keepdims=False)


def attend(queries, keyval, length):
    row_count = queries.shape[0]
    pair_count = keyval.shape[1] // (2 * HEAD_DIM)
    group_size = queries.shape[1] // (HEAD_DIM * pair_count)
    query_heads = queries.reshape(row_count, pair_count, group_size, HEAD_DIM)
    pairs = keyval.reshape(row_count, pair_count, 2, HEAD_DIM)
    scores = jnp.einsum(
        "ighd,jgd->ghij", query_heads, pairs[:, :, 0], preferred_element_type=jnp.float32
    ) * HEAD_DIM ** (-0.5)
    position = jnp.arange(row_count)
    allowed = (position[None, :] <= position[:, None]) & (position[None, :] < length)
    scores = jnp.where(allowed, scores, NEG)
    highest = jnp.max(scores, -1, keepdims=True)
    raised = jnp.exp(scores - highest)
    attn_weights = raised / jnp.sum(raised, -1, keepdims=True)
    head_mix = jnp.einsum(
        "ghij,jgd->ighd",
        attn_weights.astype(jnp.bfloat16),
        pairs[:, :, 1],
        preferred_element_type=jnp.float32,
    )
    return (head_mix.reshape(row_count, -1).astype(jnp.bfloat16), attn_weights)


def attend_back(queries, keyval, attn_weights, mix_grad):
    row_count = queries.shape[0]
    pair_count = keyval.shape[1] // (2 * HEAD_DIM)
    group_size = queries.shape[1] // (HEAD_DIM * pair_count)
    query_heads = queries.reshape(row_count, pair_count, group_size, HEAD_DIM)
    pairs = keyval.reshape(row_count, pair_count, 2, HEAD_DIM)
    grad_heads = mix_grad.reshape(row_count, pair_count, group_size, HEAD_DIM)
    value_grad = jnp.einsum(
        "ghij,ighd->jgd",
        attn_weights.astype(jnp.bfloat16),
        grad_heads,
        preferred_element_type=jnp.float32,
    ).astype(jnp.bfloat16)
    weight_grad = jnp.einsum(
        "ighd,jgd->ghij", grad_heads, pairs[:, :, 1], preferred_element_type=jnp.float32
    )
    score_grad = (
        attn_weights
        * (weight_grad - jnp.sum(weight_grad * attn_weights, -1, keepdims=True))
        * HEAD_DIM ** (-0.5)
    )
    score_grad = score_grad.astype(jnp.bfloat16)
    query_grad = (
        jnp.einsum("ghij,jgd->ighd", score_grad, pairs[:, :, 0], preferred_element_type=jnp.float32)
        .reshape(row_count, -1)
        .astype(jnp.bfloat16)
    )
    key_grad = jnp.einsum(
        "ghij,ighd->jgd", score_grad, query_heads, preferred_element_type=jnp.float32
    ).astype(jnp.bfloat16)
    return (query_grad, jnp.stack([key_grad, value_grad], 2).reshape(row_count, -1))


def window_rows(collected_items, first_step, micro_count):
    stacked = jnp.stack(collected_items)
    picked = lax.dynamic_slice_in_dim(stacked, first_step, micro_count, 0)
    return picked.reshape(micro_count * picked.shape[1], picked.shape[2])


def shards(hidden_in, lengths, gains, w_query, w_keyval, w_out, grad_out):
    sections = lax.axis_size("section")
    station = lax.axis_index("section")
    micro_count = hidden_in.shape[0]
    step_count = micro_count + sections - 1
    gain_row = gains[0]
    query_weight = w_query[0]
    model_width = query_weight.shape[0]
    pair_count = w_keyval.shape[2]
    pair_weight = w_keyval[0].reshape(model_width, -1)
    out_weight = w_out[0]
    incoming = jnp.zeros_like(hidden_in[0])
    kept_items = []
    for moment in range(step_count):
        slot_index = jnp.clip(moment - station, 0, micro_count - 1)
        own_rows = lax.dynamic_index_in_dim(hidden_in, slot_index, 0, keepdims=False)
        current = jnp.where(station == 0, own_rows, incoming)
        length = lax.dynamic_index_in_dim(lengths, slot_index, 0, keepdims=False)
        current_wide = current.astype(jnp.float32)
        scale_row = lax.rsqrt(row_sum(jnp.sum(current_wide * current_wide, -1)) / model_width + EPS)
        normed = features((current_wide * scale_row[:, None] * gain_row).astype(jnp.bfloat16))
        queries = jnp.dot(normed, query_weight, preferred_element_type=jnp.float32).astype(
            jnp.bfloat16
        )
        keyval = jnp.dot(normed, pair_weight, preferred_element_type=jnp.float32).astype(
            jnp.bfloat16
        )
        head_mix, attn_weights = attend(queries, keyval, length)
        branch = head_total(jnp.dot(head_mix, out_weight, preferred_element_type=jnp.float32))
        result = (current_wide + branch).astype(jnp.bfloat16)
        kept_items.append((current, scale_row, normed, queries, keyval, head_mix, attn_weights))
        if moment + 1 < step_count:
            incoming = neighbour(result, 1)
    past_input, past_scale, past_normed, past_queries, past_keyval, past_mix, past_weights = [
        jnp.stack(list(member_items)) for member_items in zip(*kept_items)
    ]
    incoming_grad = jnp.zeros_like(grad_out[0])
    gain_grad = jnp.zeros(gain_row.shape, jnp.float32)
    collected = []
    for moment in range(step_count):
        batch_offset = moment - (sections - 1 - station)
        is_valid = (batch_offset >= 0) & (batch_offset < micro_count)
        slot_index = jnp.clip(batch_offset, 0, micro_count - 1)
        forward_step = jnp.clip(batch_offset + station, 0, step_count - 1)
        own_grad = lax.dynamic_index_in_dim(grad_out, slot_index, 0, keepdims=False)
        current_grad = jnp.where(station == sections - 1, own_grad, incoming_grad)
        current = select_step(past_input, forward_step)
        scale_row = select_step(past_scale, forward_step)
        normed = select_step(past_normed, forward_step)
        queries = select_step(past_queries, forward_step)
        keyval = select_step(past_keyval, forward_step)
        head_mix = select_step(past_mix, forward_step)
        attn_weights = select_step(past_weights, forward_step)
        full_grad = features(current_grad)
        mix_grad = outer_side(full_grad, out_weight).astype(jnp.bfloat16)
        query_grad, pair_grad = attend_back(queries, keyval, attn_weights, mix_grad)
        normed_grad = head_total(
            outer_side(query_grad, query_weight) + outer_side(pair_grad, pair_weight)
        )
        current_wide = current.astype(jnp.float32)
        correction = row_sum(jnp.sum(normed_grad * gain_row * current_wide, -1))
        gain_step = jnp.sum(normed_grad * current_wide * scale_row[:, None], 0)
        gain_grad = gain_grad + jnp.where(is_valid, gain_step, 0.0)
        input_grad = (
            current_grad.astype(jnp.float32)
            + scale_row[:, None] * gain_row * normed_grad
            - current_wide * (scale_row**3 / model_width)[:, None] * correction[:, None]
        ).astype(jnp.bfloat16)
        collected.append((normed, query_grad, pair_grad, head_mix, full_grad))
        if moment + 1 < step_count:
            incoming_grad = neighbour(input_grad, -1)
    first_step = sections - 1 - station
    normed_rows, qgrad_rows, pgrad_rows, mixed_rows, outgrad_rows = [
        window_rows(list(member_items), first_step, micro_count) for member_items in zip(*collected)
    ]
    grad_terms = (
        inner(normed_rows, qgrad_rows),
        inner(normed_rows, pgrad_rows),
        inner(mixed_rows, outgrad_rows),
        gain_grad,
    )
    query_total, pair_total, output_total, gain_total = (
        lax.psum_scatter(grad_terms[0], "dp", scatter_dimension=0, tiled=True),
        lax.psum_scatter(grad_terms[1], "dp", scatter_dimension=0, tiled=True),
        lax.psum_scatter(grad_terms[2], "dp", scatter_dimension=1, tiled=True),
        lax.psum_scatter(grad_terms[3], "dp", scatter_dimension=0, tiled=True),
    )
    grad_query = query_total[None]
    grad_keyval = pair_total.reshape(1, pair_total.shape[0], pair_count, 2 * HEAD_DIM)
    grad_outproj = output_total[None]
    grad_gain = gain_total[None]
    return (grad_query, grad_keyval, grad_outproj, grad_gain)


def solution(mesh):
    in_specs = (
        P("dp", None, "tensor"),
        P("dp"),
        P("section", "tensor"),
        P("section", None, "tensor"),
        P("section", None, "tensor", None),
        P("section", "tensor", None),
        P("dp", None, "tensor"),
    )
    out_specs = (
        P("section", "dp", "tensor"),
        P("section", "dp", "tensor", None),
        P("section", "tensor", "dp"),
        P("section", ("tensor", "dp")),
    )
    return jax.shard_map(shards, mesh=mesh, in_specs=in_specs, out_specs=out_specs, check_vma=False)
```

profile of v0, /device:TPU:0, one launch (start us, length us, event | category | flops | bytes accessed | tf_op | source)
XLA Modules:
  0.0 1385.4 jit_solution(13235452563730377220)
XLA Ops:
  8.4 5.8 psum.63
  18.7 7.9 all_gather.30
  26.6 9.5 bitcast_dynamic-update-slice_fusion.22
  36.2 9.5 copy.264
  45.8 5.6 bitcast_dynamic-update-slice_fusion.27
  55.3 9.8 fusion.26
  65.8 21.3 %reduce-scatter.13.cloned.1.call-done = f32[64,2048]{1,0:T(8,128)} async-done(((f32[64,4096]{1,0:T(8,128)}), f32[64,2048]{1,0:T(8,128)}) %reduce-scatter.13.cloned.1.call-update) | async-done | bytes 524304 | tf_op jit(solution)/shard_map/reduce_scatter | solution.py:28
  91.8 5.4 collective-permute-done
  97.4 4.9 psum.64
  103.0 7.3 all_gather.31
  110.3 5.8 bitcast_dynamic-update-slice_fusion.26
  116.1 9.5 bitcast_dynamic-update-slice_fusion.21
  131.0 9.8 fusion.24
  140.8 21.4 %reduce-scatter.15.cloned.1.call-done = f32[64,2048]{1,0:T(8,128)} async-done(((f32[64,4096]{1,0:T(8,128)}), f32[64,2048]{1,0:T(8,128)}) %reduce-scatter.15.cloned.1.call-update) | async-done | bytes 524304 | tf_op jit(solution)/shard_map/reduce_scatter | solution.py:28
  178.2 7.5 all_gather.32
  185.7 5.8 bitcast_dynamic-update-slice_fusion.25
  191.5 9.5 bitcast_dynamic-update-slice_fusion.20
  206.4 9.8 fusion.22
  216.2 21.4 %reduce-scatter.17.cloned.1.call-done = f32[64,2048]{1,0:T(8,128)} async-done(((f32[64,4096]{1,0:T(8,128)}), f32[64,2048]{1,0:T(8,128)}) %reduce-scatter.17.cloned.1.call-update) | async-done | bytes 524304 | tf_op jit(solution)/shard_map/reduce_scatter | solution.py:28
  253.5 7.2 all_gather.33
  260.8 5.8 bitcast_dynamic-update-slice_fusion.24
  266.6 9.5 bitcast_dynamic-update-slice_fusion.19
  279.6 9.8 fusion.20
  289.5 7.0 all-gather
  297.4 11.0 fusion.63
  322.6 5.0 psum.67
  328.3 7.5 all_gather.34
  335.8 5.8 bitcast_dynamic-update-slice_fusion.23
  341.6 9.6 bitcast_dynamic-update-slice_fusion.18
  374.2 11.1 fusion.36
  385.3 7.2 convolution_add_fusion.4
  393.9 20.0 %reduce-scatter.21.cloned.1.call-done = f32[64,2048]{1,0:T(8,128)} async-done(((f32[64,4096]{1,0:T(8,128)}), f32[64,2048]{1,0:T(8,128)}) %reduce-scatter.21.cloned.1.call-update) | async-done | bytes 524304 | tf_op jit(solution)/shard_map/reduce_scatter | solution.py:28
  415.3 4.9 psum.68
  426.5 5.0 collective-permute-done.4
  432.5 7.0 all_gather.36
  440.4 11.7 fusion.66
  469.4 11.1 fusion.34
  480.5 7.0 convolution_add_fusion.3
  487.6 19.5 %reduce-scatter.23.cloned.1.call-done = f32[64,2048]{1,0:T(8,128)} async-done(((f32[64,4096]{1,0:T(8,128)}), f32[64,2048]{1,0:T(8,128)}) %reduce-scatter.23.cloned.1.call-update) | async-done | bytes 524304 | tf_op jit(solution)/shard_map/reduce_scatter | solution.py:28
  509.0 5.5 psum.69
  526.8 7.5 all_gather.37
  535.0 11.7 fusion.69
  564.0 11.1 fusion.32
  575.1 7.0 convolution_add_fusion.2
  585.0 16.7 %reduce-scatter.25.cloned.1.call-done = f32[64,2048]{1,0:T(8,128)} async-done(((f32[64,4096]{1,0:T(8,128)}), f32[64,2048]{1,0:T(8,128)}) %reduce-scatter.25.cloned.1.call-update) | async-done | bytes 524304 | tf_op jit(solution)/shard_map/reduce_scatter | solution.py:28
  603.6 5.6 psum.70
  621.5 7.0 all_gather.38
  628.5 11.8 fusion.72
  652.0 11.1 fusion.30
  663.1 7.1 convolution_add_fusion.1
  674.9 14.9 %reduce-scatter.27.cloned.1.call-done = f32[64,2048]{1,0:T(8,128)} async-done(((f32[64,4096]{1,0:T(8,128)}), f32[64,2048]{1,0:T(8,128)}) %reduce-scatter.27.cloned.1.call-update) | async-done | bytes 524304 | tf_op jit(solution)/shard_map/reduce_scatter | solution.py:28
  691.7 5.8 psum.71
  709.7 7.0 all_gather.39
  716.7 11.1 fusion.75
  735.0 10.9 fusion.28
  746.0 7.2 convolution_add_fusion
  760.4 9.1 convolution_bitcast_fusion.2
  780.1 21.4 %convolution_bitcast_fusion.1 = f32[4096,2048]{1,0:T(8,128)} fusion(bf16[5,64,4096]{2,1,0:T(8,128)(2,1)S(1)} %dynamic-slice_dynamic-update-slice_fusion, s32[]{:T(128)S(6)} %select_n.178, bf16[5,64,2048]{2,1,0:T(8,128)(2,1)} %constant_dynamic-update-slice_fusion.1), kind=kOutput, calls=%fused_computation.11 | convolution fusion | flops 2147483648 | bytes 35128320 | tf_op jit(solution)/shard_map/dot_general | solution.py:36
  807.4 13.4 convolution_bitcast_fusion
  824.8 6.5 all-reduce
  831.9 70.4 %reduce-scatter.31.cloned.1.call-done = f32[1024,1024]{1,0:T(8,128)} async-done(((f32[4096,1024]{1,0:T(8,128)}), f32[1024,1024]{1,0:T(8,128)}) %reduce-scatter.31.cloned.1.call-update) | async-done | bytes 4194320 | tf_op jit(solution)/shard_map/reduce_scatter | solution.py:197
  902.3 5.6 reshape.391
  907.9 232.4 %reduce-scatter.29.cloned.1.call-done = f32[1024,2048]{1,0:T(8,128)} async-done(((f32[4096,2048]{1,0:T(8,128)}), f32[1024,2048]{1,0:T(8,128)}) %reduce-scatter.29.cloned.1.call-update) | async-done | bytes 8388624 | tf_op jit(solution)/shard_map/reduce_scatter | solution.py:196
  1140.2 237.8 %reduce-scatter.33.cloned.1.call-done = f32[2048,1024]{1,0:T(8,128)} async-done(((f32[2048,4096]{1,0:T(8,128)}), f32[2048,1024]{1,0:T(8,128)}) %reduce-scatter.33.cloned.1.call-update) | async-done | bytes 8388624 | tf_op jit(solution)/shard_map/reduce_scatter | solution.py:198
  (403 shorter events, 242.5 us)
Async XLA Ops:
  7.2 79.9 %reduce-scatter.13.cloned.1.call-start = ((), (), s32[]{:S(2)}) async-start(), calls=%async_computation.12 | async-start | bytes 1572864 | tf_op jit(solution)/shard_map/reduce_scatter | solution.py:28
  55.3 31.8 %copy-start.6 = (bf16[2,64,2048]{2,1,0:T(8,128)(2,1)S(1)}, bf16[2,64,2048]{2,1,0:T(8,128)(2,1)}, u32[]{:S(2)}) copy-start(bf16[2,64,2048]{2,1,0:T(8,128)(2,1)} %param.7) | copy-start | bytes 1572868
  65.1 97.1 %reduce-scatter.15.cloned.1.call-start = ((), (), s32[]{:S(2)}) async-start(), calls=%async_computation.13 | async-start | bytes 1572864 | tf_op jit(solution)/shard_map/reduce_scatter | solution.py:28
  88.2 8.9 collective-permute-start
  110.3 5.8 copy-start
  130.8 10.0 copy-start.24
  140.8 96.8 %reduce-scatter.17.cloned.1.call-start = ((), (), s32[]{:S(2)}) async-start(), calls=%async_computation.14 | async-start | bytes 1572864 | tf_op jit(solution)/shard_map/reduce_scatter | solution.py:28
  163.4 8.9 collective-permute-start.1
  185.6 5.8 copy-start.1
  206.2 10.0 copy-start.26
  216.2 96.0 %reduce-scatter.19.cloned.1.call-start = ((), (), s32[]{:S(2)}) async-start(), calls=%async_computation.15 | async-start | bytes 1572864 | tf_op jit(solution)/shard_map/reduce_scatter | solution.py:28
  238.7 8.9 collective-permute-start.2
  247.7 18.8 %copy-start.8 = (bf16[5,64,2048]{2,1,0:T(8,128)(2,1)}, bf16[5,64,2048]{2,1,0:T(8,128)(2,1)S(1)}, u32[]{:S(2)}) copy-start(bf16[5,64,2048]{2,1,0:T(8,128)(2,1)S(1)} %get-tuple-element.22) | copy-start | bytes 3932164
  260.8 5.8 copy-start.3
  279.6 9.9 copy-start.19
  289.4 124.5 %reduce-scatter.21.cloned.1.call-start = ((), (), s32[]{:S(2)}) async-start(), calls=%async_computation.16 | async-start | bytes 1572864 | tf_op jit(solution)/shard_map/reduce_scatter | solution.py:28
  297.4 12.6 copy-start.64
  297.4 13.7 copy-start.66
  308.4 9.4 copy-start.68
  310.0 50.1 %copy-start.59 = (pred[64,64]{0,1:T(8,128)(4,1)}, pred[64,64]{0,1:T(8,128)(4,1)S(1)}, u32[]{:S(2)}) copy-start(pred[64,64]{0,1:T(8,128)(4,1)S(1)} %fusion.295) | copy-start | bytes 12292
  312.2 9.5 copy-start.7
  313.4 8.3 collective-permute-start.3
  335.8 5.9 copy-start.5
  335.8 5.9 copy-start.38
  341.6 9.6 copy-start.44
  371.4 13.8 copy-start.30
  374.2 11.1 copy-start.50
  385.3 7.3 copy-start.69
  385.3 7.3 copy-start.70
  392.5 31.2 %copy-start.48 = (bf16[1,64,1024]{2,1,0:T(8,128)(2,1)S(1)}, bf16[1,64,1024]{2,1,0:T(8,128)(2,1)}, u32[]{:S(2)}) copy-start(bf16[1,64,1024]{2,1,0:T(8,128)(2,1)} %get-tuple-element.36) | copy-start | bytes 393220
  392.5 114.6 %reduce-scatter.23.cloned.1.call-start = ((), (), s32[]{:S(2)}) async-start(), calls=%async_computation.17 | async-start | bytes 1572864 | tf_op jit(solution)/shard_map/reduce_scatter | solution.py:28
  393.3 30.4 %copy-start.61 = (f32[5,64]{1,0:T(8,128)}, f32[5,64]{1,0:T(8,128)S(1)}, u32[]{:S(2)}) copy-start(f32[5,64]{1,0:T(8,128)S(1)} %stack.228) | copy-start | bytes 3844
  422.4 9.1 collective-permute-start.4
  469.4 11.1 copy-start.51
  487.5 114.2 %reduce-scatter.25.cloned.1.call-start = ((), (), s32[]{:S(2)}) async-start(), calls=%async_computation.18 | async-start | bytes 1572864 | tf_op jit(solution)/shard_map/reduce_scatter | solution.py:28
  516.6 9.1 collective-permute-start.5
  564.0 11.1 copy-start.52
  582.2 107.6 %reduce-scatter.27.cloned.1.call-start = ((), (), s32[]{:S(2)}) async-start(), calls=%async_computation.19 | async-start | bytes 1572864 | tf_op jit(solution)/shard_map/reduce_scatter | solution.py:28
  583.1 29.7 %copy-start.2 = (bf16[64,4096]{1,0:T(8,128)(2,1)S(1)}, bf16[64,4096]{1,0:T(8,128)(2,1)}, u32[]{:S(2)}) copy-start(bf16[64,4096]{1,0:T(8,128)(2,1)} %copy-done.1) | copy-start | bytes 1572868
  611.3 9.1 collective-permute-start.6
  628.5 11.8 copy-start.15
  649.3 2.8 copy-start.34
  652.0 11.1 copy-start.53
  663.1 7.2 copy-start.4
  670.3 153.2 %reduce-scatter.35.cloned.1.call-start = ((), (), s32[]{:S(2)}) async-start(), calls=%async_computation.23 | async-start | bytes 1572864 | tf_op jit(solution)/shard_map/reduce_scatter | solution.py:28
  674.9 33.8 %copy-start.20 = (bf16[2,64,2048]{2,1,0:T(8,128)(2,1)S(1)}, bf16[2,64,2048]{2,1,0:T(8,128)(2,1)}, u32[]{:S(2)}) copy-start(bf16[2,64,2048]{2,1,0:T(8,128)(2,1)} %param.13) | copy-start | bytes 1572868
  699.6 9.1 collective-permute-start.7
  716.7 11.1 copy-start.17
  734.5 11.4 copy-start.36
  745.9 7.6 copy-start.49
  745.9 8.2 copy-start.21
  753.2 4.3 copy-start.39
  753.2 5.0 copy-start.40
  753.2 5.8 copy-start.42
  753.2 149.1 %reduce-scatter.31.cloned.1.call-start = ((), (), s32[]{:S(2)}) async-start(), calls=%async_computation.21 | async-start | bytes 20971520 | tf_op jit(solution)/shard_map/reduce_scatter | solution.py:197
  769.5 3.5 copy-start.32
  769.5 6.1 copy-start.33
  769.6 370.7 %reduce-scatter.29.cloned.1.call-start = ((), (), s32[]{:S(2)}) async-start(), calls=%async_computation.20 | async-start | bytes 41943040 | tf_op jit(solution)/shard_map/reduce_scatter | solution.py:196
  771.4 6.9 copy-start.35
  774.0 5.2 copy-start.37
  801.6 576.5 %reduce-scatter.33.cloned.1.call-start = ((), (), s32[]{:S(2)}) async-start(), calls=%async_computation.22 | async-start | bytes 41943040 | tf_op jit(solution)/shard_map/reduce_scatter | solution.py:198
  820.9 3.8 copy-start.56
  820.9 3.8 copy-start.57
  820.9 3.9 copy-start.58
  (28 other events, 41.7 us)
Sparse Core Ops, SparseCore 0:
  65.3 21.7 reduce-scatter.12
  140.9 21.3 reduce-scatter.14
  216.3 21.2 reduce-scatter.16
  289.5 21.3 reduce-scatter.18
  392.6 21.2 reduce-scatter.20
  487.7 19.3 reduce-scatter.22
  582.3 19.3 reduce-scatter.24
  670.4 19.3 reduce-scatter.26
  753.3 19.8 reduce-scatter.34
  775.8 126.3 reduce-scatter.30
  905.4 234.7 reduce-scatter.28
  1143.3 234.7 reduce-scatter.32
where the time goes:
time: 1400 us; the launch traced here: 1390 us
  waiting for transfers between devices  707 us (50%)
  matrix products  361 us (26%)
  blocking collectives  127 us (9%)
  local copies, waits for them, and re-layouts  107 us (8%)
  other arithmetic  46.6 us (3%)
  starting transfers between devices  20.7 us (1%)
  between operations  16.7 us (1%)
    reduce_scatter x1, waiting for transfers between devices, shards(): lax.psum_scatter(grad_terms[2], 'dp', scatter_dimension=1, tiled=True)  238 us
    reduce_scatter x1, waiting for transfers between devices, shards(): lax.psum_scatter(grad_terms[0], 'dp', scatter_dimension=0, tiled=True)  232 us
    dot_general x15, matrix products, outer_side(): lax.dot_general(former, latter, (((1,), (1,)), ((), ())), preferred_eleme...  148 us
    reduce_scatter x9, waiting for transfers between devices, head_total(): return lax.psum_scatter(operand, 'tensor', scatter_dimension=1, tiled=True)  135 us
    all_gather x10, blocking collectives, features(): return lax.all_gather(operand, 'tensor', axis=1, tiled=True)  72.9 us
    reduce_scatter x1, waiting for transfers between devices, shards(): lax.psum_scatter(grad_terms[1], 'dp', scatter_dimension=0, tiled=True)  70.4 us
    dot_general x5, matrix products, shards(): jnp.dot(normed, query_weight, preferred_element_type=jnp.float32)  47.6 us
    psum x9, blocking collectives, row_sum(): return lax.psum(operand, 'tensor')  47.6 us
  transfers between devices with their start and end apart: 20, of which 18 were waited for; matrix products, arithmetic and copies ran while one was open for 8% of the time, Pallas kernels for 0%

commit v1 on v0

--- a/solution.py
+++ b/solution.py
@@ -20,12 +20,47 @@
     return lax.all_gather(operand, "tensor", axis=1, tiled=True)
 
 
-def row_sum(operand):
-    return lax.psum(operand, "tensor")
-
-
 def head_total(operand):
-    return lax.psum_scatter(operand, "tensor", scatter_dimension=1, tiled=True)
+    ranks = lax.axis_size("tensor")
+    rank = lax.axis_index("tensor")
+    width = operand.shape[1] // ranks
+    total = lax.dynamic_slice_in_dim(operand, rank * width, width, 1)
+    for distance in range(1, ranks):
+        target = lax.rem(rank + distance, ranks)
+        block = lax.dynamic_slice_in_dim(operand, target * width, width, 1).astype(jnp.bfloat16)
+        route = [(i, (i + distance) % ranks) for i in range(ranks)]
+        total = total + lax.ppermute(block, "tensor", route).astype(jnp.float32)
+    return total
+
+
+def replica_bits():
+    ranks = lax.axis_size("dp")
+    return [1 << power for power in reversed(range(ranks.bit_length() - 1))]
+
+
+def exchange(block, mask):
+    return lax.ppermute(block, "dp", [(i, i ^ mask) for i in range(lax.axis_size("dp"))])
+
+
+def every_row(block):
+    for bit in replica_bits():
+        block = jnp.concatenate([block, exchange(block, bit)], 0)
+    return block
+
+
+def own_columns(block):
+    ranks = lax.axis_size("dp")
+    rank = lax.axis_index("dp")
+    width = block.shape[1] // ranks
+    masks = [0]
+    for bit in replica_bits():
+        masks = masks + [mask ^ bit for mask in masks]
+    pieces = []
+    for mask in masks:
+        target = jnp.bitwise_xor(rank, mask)
+        piece = lax.dynamic_slice_in_dim(block, target * width, width, 1)
+        pieces.append(exchange(piece, mask) if mask else piece)
+    return jnp.concatenate(pieces, 0)
 
 
 def neighbour(operand, offset):
@@ -105,8 +140,7 @@
     return (query_grad, jnp.stack([key_grad, value_grad], 2).reshape(row_count, -1))
 
 
-def window_rows(collected_items, first_step, micro_count):
-    stacked = jnp.stack(collected_items)
+def window_rows(stacked, first_step, micro_count):
     picked = lax.dynamic_slice_in_dim(stacked, first_step, micro_count, 0)
     return picked.reshape(micro_count * picked.shape[1], picked.shape[2])
 
@@ -117,6 +151,7 @@
     micro_count = hidden_in.shape[0]
     step_count = micro_count + sections - 1
     gain_row = gains[0]
+    gain_full = features(gains)[0].astype(jnp.float32)
     query_weight = w_query[0]
     model_width = query_weight.shape[0]
     pair_count = w_keyval.shape[2]
@@ -130,8 +165,10 @@
         current = jnp.where(station == 0, own_rows, incoming)
         length = lax.dynamic_index_in_dim(lengths, slot_index, 0, keepdims=False)
         current_wide = current.astype(jnp.float32)
-        scale_row = lax.rsqrt(row_sum(jnp.sum(current_wide * current_wide, -1)) / model_width + EPS)
-        normed = features((current_wide * scale_row[:, None] * gain_row).astype(jnp.bfloat16))
+        current_full = features(current)
+        full_wide = current_full.astype(jnp.float32)
+        scale_row = lax.rsqrt(jnp.sum(full_wide * full_wide, -1) / model_width + EPS)
+        normed = (full_wide * scale_row[:, None] * gain_full).astype(jnp.bfloat16)
         queries = jnp.dot(normed, query_weight, preferred_element_type=jnp.float32).astype(
             jnp.bfloat16
         )
@@ -141,12 +178,14 @@
         head_mix, attn_weights = attend(queries, keyval, length)
         branch = head_total(jnp.dot(head_mix, out_weight, preferred_element_type=jnp.float32))
         result = (current_wide + branch).astype(jnp.bfloat16)
-        kept_items.append((current, scale_row, normed, queries, keyval, head_mix, attn_weights))
+        kept_items.append((current, current_full, scale_row, normed, queries, keyval, head_mix, attn_weights))
         if moment + 1 < step_count:
             incoming = neighbour(result, 1)
-    past_input, past_scale, past_normed, past_queries, past_keyval, past_mix, past_weights = [
+    past_input, past_full, past_scale, past_normed, past_queries, past_keyval, past_mix, past_weights = [
         jnp.stack(list(member_items)) for member_items in zip(*kept_items)
     ]
+    normed_rows = own_columns(window_rows(past_normed, station, micro_count))
+    mixed_rows = every_row(window_rows(past_mix, station, micro_count))
     incoming_grad = jnp.zeros_like(grad_out[0])
     gain_grad = jnp.zeros(gain_row.shape, jnp.float32)
     collected = []
@@ -159,19 +198,17 @@
         current_grad = jnp.where(station == sections - 1, own_grad, incoming_grad)
         current = select_step(past_input, forward_step)
         scale_row = select_step(past_scale, forward_step)
-        normed = select_step(past_normed, forward_step)
+        current_full = select_step(past_full, forward_step).astype(jnp.float32)
         queries = select_step(past_queries, forward_step)
         keyval = select_step(past_keyval, forward_step)
-        head_mix = select_step(past_mix, forward_step)
         attn_weights = select_step(past_weights, forward_step)
         full_grad = features(current_grad)
         mix_grad = outer_side(full_grad, out_weight).astype(jnp.bfloat16)
         query_grad, pair_grad = attend_back(queries, keyval, attn_weights, mix_grad)
-        normed_grad = head_total(
-            outer_side(query_grad, query_weight) + outer_side(pair_grad, pair_weight)
-        )
+        partial_grad = outer_side(query_grad, query_weight) + outer_side(pair_grad, pair_weight)
+        correction = lax.psum(jnp.sum(partial_grad * gain_full * current_full, -1), "tensor")
+        normed_grad = head_total(partial_grad)
         current_wide = current.astype(jnp.float32)
-        correction = row_sum(jnp.sum(normed_grad * gain_row * current_wide, -1))
         gain_step = jnp.sum(normed_grad * current_wide * scale_row[:, None], 0)
         gain_grad = gain_grad + jnp.where(is_valid, gain_step, 0.0)
         input_grad = (
@@ -179,25 +216,20 @@
             + scale_row[:, None] * gain_row * normed_grad
             - current_wide * (scale_row**3 / model_width)[:, None] * correction[:, None]
         ).astype(jnp.bfloat16)
-        collected.append((normed, query_grad, pair_grad, head_mix, full_grad))
+        collected.append((jnp.concatenate([query_grad, pair_grad], 1), full_grad))
         if moment + 1 < step_count:
             incoming_grad = neighbour(input_grad, -1)
     first_step = sections - 1 - station
-    normed_rows, qgrad_rows, pgrad_rows, mixed_rows, outgrad_rows = [
-        window_rows(list(member_items), first_step, micro_count) for member_items in zip(*collected)
+    pair_rows, outgrad_rows = [
+        window_rows(jnp.stack(list(member_items)), first_step, micro_count)
+        for member_items in zip(*collected)
     ]
-    grad_terms = (
-        inner(normed_rows, qgrad_rows),
-        inner(normed_rows, pgrad_rows),
-        inner(mixed_rows, outgrad_rows),
-        gain_grad,
-    )
-    query_total, pair_total, output_total, gain_total = (
-        lax.psum_scatter(grad_terms[0], "dp", scatter_dimension=0, tiled=True),
-        lax.psum_scatter(grad_terms[1], "dp", scatter_dimension=0, tiled=True),
-        lax.psum_scatter(grad_terms[2], "dp", scatter_dimension=1, tiled=True),
-        lax.psum_scatter(grad_terms[3], "dp", scatter_dimension=0, tiled=True),
-    )
+    output_total = inner(mixed_rows, own_columns(outgrad_rows))
+    pair_rows = every_row(pair_rows)
+    query_width = query_weight.shape[1]
+    query_total = inner(normed_rows, pair_rows[:, :query_width])
+    pair_total = inner(normed_rows, pair_rows[:, query_width:])
+    gain_total = lax.psum_scatter(gain_grad, "dp", scatter_dimension=0, tiled=True)
     grad_query = query_total[None]
     grad_keyval = pair_total.reshape(1, pair_total.shape[0], pair_count, 2 * HEAD_DIM)
     grad_outproj = output_total[None]

time: 1400 us -> 732 us (0.52)
  waiting for transfers between devices: 707 us -> 39.3 us
  starting transfers between devices: 20.7 us -> 39.3 us
  matrix products: 361 us -> 343 us
  local copies, waits for them, and re-layouts: 107 us -> 122 us
    reduce_scatter x12 -> x0, waiting for transfers between devices: 676 us -> none  [the longest x1 238 us: shards(): lax.psum_scatter(grad_terms[2], 'dp', scatter_dimension=1, tiled=True)]
    dot_general x3, matrix products: 44 us -> 17.6 us  [inner(): lax.dot_general(former, latter, (((0,), (0,)), ((), ())), preferred_eleme...]
    psum x9 -> x4, blocking collectives: 47.6 us -> 22.1 us  [shards(): lax.psum(jnp.sum(partial_grad * gain_full * current_full, -1), 'tensor')]
    ppermute x0 -> x19, waiting for transfers between devices: none -> 19 us  [the longest x9 9.53 us: head_total(): total = total + lax.ppermute(block, 'tensor', route).astype(jnp.float32)]
    ppermute x0 -> x19, starting transfers between devices: none -> 16.9 us  [the longest x9 10.8 us: head_total(): total = total + lax.ppermute(block, 'tensor', route).astype(jnp.float32)]
    all_gather x10 -> x11, blocking collectives: 72.9 us -> 81.8 us  [features(): return lax.all_gather(operand, 'tensor', axis=1, tiled=True)]
    unnamed x175 -> x176, local copies, waits for them, and re-layouts: 40.5 us -> 34.9 us
  transfers between devices with their start and end apart: 20 -> 27, of which waited for: 18 -> 11; matrix products, arithmetic and copies ran while one was open for 8% -> 35% of each run, Pallas kernels for 0% -> 0%
where the time goes in v1:
time: 732 us; the launch traced here: 721 us
  matrix products  343 us (47%)
  local copies, waits for them, and re-layouts  122 us (17%)
  blocking collectives  117 us (16%)
  other arithmetic  57.6 us (8%)
  starting transfers between devices  39.3 us (5%)
  waiting for transfers between devices  39.3 us (5%)
    dot_general x15, matrix products, outer_side(): lax.dot_general(former, latter, (((1,), (1,)), ((), ())), preferred_eleme...  149 us
    all_gather x11, blocking collectives, features(): return lax.all_gather(operand, 'tensor', axis=1, tiled=True)  81.8 us
    dot_general x5, matrix products, shards(): jnp.dot(normed, query_weight, preferred_element_type=jnp.float32)  48.3 us
    dot_general x4, matrix products, shards(): jnp.dot(head_mix, out_weight, preferred_element_type=jnp.float32)  35.5 us
    unnamed x176, local copies, waits for them, and re-layouts  34.9 us
    dot_general x5, matrix products, shards(): jnp.dot(normed, pair_weight, preferred_element_type=jnp.float32)  28.5 us
    ppermute x8, starting transfers between devices, shifted(): return lax.ppermute(block, axis, route)  22.4 us
    psum x4, blocking collectives, shards(): lax.psum(jnp.sum(partial_grad * gain_full * current_full, -1), 'tensor')  22.1 us
  transfers between devices with their start and end apart: 27, of which 11 were waited for; matrix products, arithmetic and copies ran while one was open for 35% of the time, Pallas kernels for 0%

profile of v1, /device:TPU:0, one launch (start us, length us, event | category | flops | bytes accessed | tf_op | source)
XLA Modules:
  0.0 721.1 jit_solution(6193339774076245101)
XLA Ops:
  2.4 9.9 %all-gather = bf16[1,64,4096]{2,1,0:T(8,128)(2,1)S(1)} all-gather(bf16[1,64,2048]{2,1,0:T(8,128)(2,1)S(1)} %get-tuple-element.35), channel_id=2, replica_groups=mesh['section'=4,'tensor'=2,'dp'=4] {'tensor'}, dimensions={2}, use_global_device_ids=true | all-gather | bytes 786432 | tf_op jit(solution)/shard_map/all_gather | solution.py:20
  13.0 4.6 all_gather.34
  17.6 9.5 %copy.247 = bf16[512,8,4,256]{3,1,2,0:T(8,128)(2,1)} copy(bf16[512,8,4,256]{3,2,1,0:T(4,128)(2,1)} %bitcast.753) | data formatting | bytes 16777216
  27.1 5.7 bitcast_dynamic-update-slice_fusion.31
  33.1 9.6 %bitcast_dynamic-update-slice_fusion.26 = (bf16[5,64,2048]{2,1,0:T(8,128)(2,1)}, bf16[64,2048]{1,0:T(8,128)(2,1)S(1)}) fusion(bf16[1,4096,2048]{2,1,0:T(8,128)(2,1)} %param.10, bf16[1,64,4096]{2,1,0:T(8,128)(2,1)S(1)} %all-gather, f32[4096]{0:T(1024)S(1)} %bitcast.735, f32[64]{0:T(128)S(1)} %get-tuple-element.101), kind=kOutput, calls=%fused_computation.357 | convolution fusion | flops 1074921472 | bytes 17842432 | tf_op jit(solution)/shard_map/dot_general | solution.py:172
  46.6 8.8 %fusion.26 = f32[64,4096]{1,0:T(8,128)S(1)} fusion(bf16[64,2048]{1,0:T(8,128)(2,1)S(1)} %convert_element_type.502, bf16[1,2048,4096]{2,1,0:T(8,128)(2,1)} %param.12), kind=kOutput, calls=%fused_computation.26 | convolution fusion | flops 1073741824 | bytes 18087936 | tf_op jit(solution)/shard_map/dot_general | solution.py:179
  59.2 9.3 %all-gather.1 = bf16[1,64,4096]{2,1,0:T(8,128)(2,1)S(1)} all-gather(bf16[1,64,2048]{2,1,0:T(8,128)(2,1)S(1)} %dynamic-slice_select_fusion), channel_id=3, replica_groups=mesh['section'=4,'tensor'=2,'dp'=4] {'tensor'}, dimensions={2}, use_global_device_ids=true | all-gather | bytes 786432 | tf_op jit(solution)/shard_map/all_gather | solution.py:20
  68.5 10.9 %fusion.63 = bf16[64,2048]{1,0:T(8,128)(2,1)S(1)} fusion(bf16[1,2048,4096]{2,1,0:T(8,128)(2,1)} %param.12, bf16[1,64,4096]{2,1,0:T(8,128)(2,1)S(1)} %all-gather.1), kind=kOutput, calls=%fused_computation.61 | convolution fusion | flops 1073872896 | bytes 17563648 | tf_op jit(solution)/shard_map/dot_general | solution.py:77
  86.6 3.7 collective-permute-start.1
  96.4 7.0 all_gather.35
  104.2 5.7 bitcast_dynamic-update-slice_fusion.30
  111.8 9.7 %bitcast_dynamic-update-slice_fusion.25 = (bf16[5,64,2048]{2,1,0:T(8,128)(2,1)}, bf16[64,2048]{1,0:T(8,128)(2,1)}) fusion(bf16[5,64,2048]{2,1,0:T(8,128)(2,1)} %get-tuple-element.127, bf16[1,4096,2048]{2,1,0:T(8,128)(2,1)} %param.10, bf16[64,4096]{1,0:T(8,128)(2,1)S(1)} %all_gather.35, f32[64]{0:T(128)} %copy-done.55, f32[4096]{0:T(1024)S(1)} %bitcast.738), kind=kOutput, calls=%fused_computation.356 | convolution fusion | flops 1074921472 | bytes 17842688 | tf_op jit(solution)/shard_map/dot_general | solution.py:172
  134.4 8.9 %fusion.24 = f32[64,4096]{1,0:T(8,128)S(1)} fusion(bf16[64,2048]{1,0:T(8,128)(2,1)} %convert_element_type.514, bf16[1,2048,4096]{2,1,0:T(8,128)(2,1)} %param.12), kind=kOutput, calls=%fused_computation.24 | convolution fusion | flops 1073741824 | bytes 18087936 | tf_op jit(solution)/shard_map/dot_general | solution.py:179
  148.5 3.2 collective-permute-done.2
  152.9 4.8 collective-permute-start.3
  163.3 7.4 %all_gather.36 = bf16[64,4096]{1,0:T(8,128)(2,1)S(1)} all-gather(bf16[64,2048]{1,0:T(8,128)(2,1)S(1)} %get-tuple-element.31), channel_id=1, replica_groups=mesh['section'=4,'tensor'=2,'dp'=4] {'tensor'}, dimensions={1}, use_global_device_ids=true | all-gather | bytes 786432 | tf_op jit(solution)/shard_map/all_gather | solution.py:20
  171.5 5.7 bitcast_dynamic-update-slice_fusion.29
  179.2 9.7 %bitcast_dynamic-update-slice_fusion.24 = (bf16[5,64,2048]{2,1,0:T(8,128)(2,1)}, bf16[64,2048]{1,0:T(8,128)(2,1)}) fusion(bf16[5,64,2048]{2,1,0:T(8,128)(2,1)} %get-tuple-element.129, bf16[1,4096,2048]{2,1,0:T(8,128)(2,1)} %param.10, bf16[64,4096]{1,0:T(8,128)(2,1)S(1)} %all_gather.36, f32[64]{0:T(128)} %copy-done.57, f32[4096]{0:T(1024)S(1)} %bitcast.741), kind=kOutput, calls=%fused_computation.355 | convolution fusion | flops 1074921472 | bytes 17842688 | tf_op jit(solution)/shard_map/dot_general | solution.py:172
  201.7 8.9 %fusion.22 = f32[64,4096]{1,0:T(8,128)S(1)} fusion(bf16[64,2048]{1,0:T(8,128)(2,1)} %convert_element_type.526, bf16[1,2048,4096]{2,1,0:T(8,128)(2,1)} %param.12), kind=kOutput, calls=%fused_computation.22 | convolution fusion | flops 1073741824 | bytes 18087936 | tf_op jit(solution)/shard_map/dot_general | solution.py:179
  215.9 3.2 collective-permute-done.4
  220.3 4.4 collective-permute-start.5
  230.3 7.2 %all_gather.37 = bf16[64,4096]{1,0:T(8,128)(2,1)S(1)} all-gather(bf16[64,2048]{1,0:T(8,128)(2,1)S(1)} %get-tuple-element.29), channel_id=1, replica_groups=mesh['section'=4,'tensor'=2,'dp'=4] {'tensor'}, dimensions={1}, use_global_device_ids=true | all-gather | bytes 786432 | tf_op jit(solution)/shard_map/all_gather | solution.py:20
  238.3 5.7 bitcast_dynamic-update-slice_fusion.28
  245.9 9.7 %bitcast_dynamic-update-slice_fusion.23 = (bf16[5,64,2048]{2,1,0:T(8,128)(2,1)}, bf16[64,2048]{1,0:T(8,128)(2,1)}) fusion(bf16[5,64,2048]{2,1,0:T(8,128)(2,1)} %get-tuple-element.131, bf16[1,4096,2048]{2,1,0:T(8,128)(2,1)} %param.10, bf16[64,4096]{1,0:T(8,128)(2,1)S(1)} %all_gather.37, f32[64]{0:T(128)} %copy-done.59, f32[4096]{0:T(1024)S(1)} %bitcast.744), kind=kOutput, calls=%fused_computation.354 | convolution fusion | flops 1074921472 | bytes 17842688 | tf_op jit(solution)/shard_map/dot_general | solution.py:172
  268.5 8.9 %fusion.20 = f32[64,4096]{1,0:T(8,128)S(1)} fusion(bf16[64,2048]{1,0:T(8,128)(2,1)} %convert_element_type.538, bf16[1,2048,4096]{2,1,0:T(8,128)(2,1)} %param.12), kind=kOutput, calls=%fused_computation.20 | convolution fusion | flops 1073741824 | bytes 18087936 | tf_op jit(solution)/shard_map/dot_general | solution.py:179
  282.6 3.2 collective-permute-done.6
  287.0 4.4 collective-permute-start.7
  297.0 7.4 %all_gather.38 = bf16[64,4096]{1,0:T(8,128)(2,1)S(1)} all-gather(bf16[64,2048]{1,0:T(8,128)(2,1)S(1)} %get-tuple-element.27), channel_id=1, replica_groups=mesh['section'=4,'tensor'=2,'dp'=4] {'tensor'}, dimensions={1}, use_global_device_ids=true | all-gather | bytes 786432 | tf_op jit(solution)/shard_map/all_gather | solution.py:20
  305.3 5.7 bitcast_dynamic-update-slice_fusion.27
  311.9 9.6 %bitcast_dynamic-update-slice_fusion.22 = (bf16[5,64,2048]{2,1,0:T(8,128)(2,1)}, bf16[64,2048]{1,0:T(8,128)(2,1)S(1)}) fusion(bf16[5,64,2048]{2,1,0:T(8,128)(2,1)} %get-tuple-element.133, bf16[1,4096,2048]{2,1,0:T(8,128)(2,1)} %param.10, bf16[64,4096]{1,0:T(8,128)(2,1)S(1)} %all_gather.38, f32[64]{0:T(128)S(1)} %get-tuple-element.93, f32[4096]{0:T(1024)S(1)} %bitcast.747), kind=kOutput, calls=%fused_computation.353 | convolution fusion | flops 1074921472 | bytes 17842432 | tf_op jit(solution)/shard_map/dot_general | solution.py:172
  322.4 2.8 fusion.439
  338.1 12.1 %fusion.36 = f32[64,4096]{1,0:T(8,128)} fusion(bf16[64,2048]{1,0:T(8,128)(2,1)S(1)} %convert_element_type.550, bf16[1,4096,2048]{2,1,0:T(8,128)(2,1)} %param.10), kind=kOutput, calls=%fused_computation.36 | convolution fusion | flops 1073741824 | bytes 18087936 | tf_op jit(solution)/shard_map/dot_general | solution.py:77
  359.1 7.0 fusion.185
  381.4 5.4 psum.28
  405.0 7.0 all_gather.40
  412.9 11.0 %fusion.66 = bf16[64,2048]{1,0:T(8,128)(2,1)S(1)} fusion(bf16[64,4096]{1,0:T(8,128)(2,1)S(1)} %all_gather.40, bf16[1,2048,4096]{2,1,0:T(8,128)(2,1)} %param.12), kind=kOutput, calls=%fused_computation.62 | convolution fusion | flops 1073872896 | bytes 17563648 | tf_op jit(solution)/shard_map/dot_general | solution.py:77
  432.4 11.9 %fusion.34 = f32[64,4096]{1,0:T(8,128)} fusion(bf16[64,2048]{1,0:T(8,128)(2,1)S(1)} %convert_element_type.568, bf16[1,4096,2048]{2,1,0:T(8,128)(2,1)} %param.10), kind=kOutput, calls=%fused_computation.34 | convolution fusion | flops 1073741824 | bytes 18087936 | tf_op jit(solution)/shard_map/dot_general | solution.py:77
  447.7 7.2 fusion.184
  458.2 5.6 psum.29
  469.8 5.0 collective-permute-done.14
  475.6 7.4 %all_gather.41 = bf16[64,4096]{1,0:T(8,128)(2,1)S(1)} all-gather(bf16[64,2048]{1,0:T(8,128)(2,1)S(1)} %bitcast_select_fusion.2), channel_id=1, replica_groups=mesh['section'=4,'tensor'=2,'dp'=4] {'tensor'}, dimensions={1}, use_global_device_ids=true | all-gather | bytes 786432 | tf_op jit(solution)/shard_map/all_gather | solution.py:20
  483.8 11.0 %fusion.69 = bf16[64,2048]{1,0:T(8,128)(2,1)S(1)} fusion(bf16[64,4096]{1,0:T(8,128)(2,1)S(1)} %all_gather.41, bf16[1,2048,4096]{2,1,0:T(8,128)(2,1)} %param.12), kind=kOutput, calls=%fused_computation.63 | convolution fusion | flops 1073872896 | bytes 17563648 | tf_op jit(solution)/shard_map/dot_general | solution.py:77
  503.4 12.0 %fusion.32 = f32[64,4096]{1,0:T(8,128)} fusion(bf16[64,2048]{1,0:T(8,128)(2,1)S(1)} %convert_element_type.586, bf16[1,4096,2048]{2,1,0:T(8,128)(2,1)} %param.10), kind=kOutput, calls=%fused_computation.32 | convolution fusion | flops 1073741824 | bytes 18087936 | tf_op jit(solution)/shard_map/dot_general | solution.py:77
  518.7 7.2 fusion.183
  529.7 5.5 psum.30
  538.9 6.2 collective-permute-done.16
  545.9 7.2 all_gather.42
  553.9 11.0 %fusion.72 = bf16[64,2048]{1,0:T(8,128)(2,1)S(1)} fusion(bf16[64,4096]{1,0:T(8,128)(2,1)S(1)} %all_gather.42, bf16[1,2048,4096]{2,1,0:T(8,128)(2,1)} %param.12), kind=kOutput, calls=%fused_computation.64 | convolution fusion | flops 1073872896 | bytes 17563648 | tf_op jit(solution)/shard_map/dot_general | solution.py:77
  573.4 12.0 %fusion.30 = f32[64,4096]{1,0:T(8,128)} fusion(bf16[64,2048]{1,0:T(8,128)(2,1)S(1)} %convert_element_type.604, bf16[1,4096,2048]{2,1,0:T(8,128)(2,1)} %param.10), kind=kOutput, calls=%fused_computation.30 | convolution fusion | flops 1073741824 | bytes 18087936 | tf_op jit(solution)/shard_map/dot_general | solution.py:77
  588.8 7.2 fusion.182
  599.3 5.6 psum.31
  608.7 3.2 fusion.210
  611.9 3.0 collective-permute-done.18
  614.9 7.3 %all_gather.43 = bf16[64,4096]{1,0:T(8,128)(2,1)S(1)} all-gather(bf16[64,2048]{1,0:T(8,128)(2,1)S(1)} %bitcast_select_fusion), channel_id=1, replica_groups=mesh['section'=4,'tensor'=2,'dp'=4] {'tensor'}, dimensions={1}, use_global_device_ids=true | all-gather | bytes 786432 | tf_op jit(solution)/shard_map/all_gather | solution.py:20
  622.2 11.0 %fusion.75 = bf16[64,2048]{1,0:T(8,128)(2,1)S(1)} fusion(bf16[64,4096]{1,0:T(8,128)(2,1)S(1)} %all_gather.43, bf16[1,2048,4096]{2,1,0:T(8,128)(2,1)} %param.12), kind=kOutput, calls=%fused_computation.65 | convolution fusion | flops 1073872896 | bytes 17563648 | tf_op jit(solution)/shard_map/dot_general | solution.py:77
  641.7 11.9 %fusion.28 = f32[64,4096]{1,0:T(8,128)} fusion(bf16[64,2048]{1,0:T(8,128)(2,1)S(1)} %convert_element_type.622, bf16[1,4096,2048]{2,1,0:T(8,128)(2,1)} %param.10), kind=kOutput, calls=%fused_computation.28 | convolution fusion | flops 1073741824 | bytes 18087936 | tf_op jit(solution)/shard_map/dot_general | solution.py:77
  658.0 6.0 convolution_add_fusion
  665.4 4.1 collective-permute-done.19
  675.2 13.0 %all-reduce = f32[2048]{0:T(1024)S(1)} all-reduce(f32[2048]{0:T(1024)S(1)} %select_add_fusion), channel_id=4, replica_groups=mesh['section'=4,'tensor'=2,'dp'=4] {'dp'}, use_global_device_ids=true, to_apply=%region_33.34.clone | all-reduce | flops 2048 | bytes 16384
  690.7 7.2 %convolution_bitcast_fusion = f32[1,2048,1024]{2,1,0:T(8,128)} fusion(bf16[256,2048]{1,0:T(8,128)(2,1)} %collective-permute-done.22, bf16[128,2048]{1,0:T(8,128)(2,1)} %collective-permute-done.21, bf16[128,2048]{1,0:T(8,128)(2,1)S(1)} %bitcast.763, bf16[128,1024]{1,0:T(8,128)(2,1)S(1)} %collective-permute-done.25, ...), kind=kOutput, calls=%fused_computation.53 | convolution fusion | flops 2157969408 | bytes 11534336 | tf_op jit(solution)/shard_map/dot_general | solution.py:71
  698.0 5.3 collective-permute-done.8
  703.3 4.5 fusion.169
  707.9 5.2 copy.186
  714.8 5.8 convolution_bitcast_fusion.1
  (407 shorter events, 250.9 us)
Async XLA Ops:
  46.6 12.5 %copy-start.6 = (bf16[2,64,2048]{2,1,0:T(8,128)(2,1)S(1)}, bf16[2,64,2048]{2,1,0:T(8,128)(2,1)}, u32[]{:S(2)}) copy-start(bf16[2,64,2048]{2,1,0:T(8,128)(2,1)} %param.13) | copy-start | bytes 1572868
  56.3 29.5 %collective-permute-start = (bf16[64,2048]{1,0:T(8,128)(2,1)}, bf16[64,2048]{1,0:T(8,128)(2,1)S(1)}, u32[]{:S(2)}, u32[]{:S(2)}) collective-permute-start(bf16[64,2048]{1,0:T(8,128)(2,1)} %dynamic-slice_convert_fusion.8), channel_id=1, source_target_pairs={{0,4},{4,0},{1,5},{5,1},{2,6},{6,2},{3,7},{7,3},{8,12},{12,8},{9,1... | collective-permute-start | bytes 786440 | tf_op jit(solution)/shard_map/ppermute | solution.py:32
  79.4 11.5 %copy-start.53 = (bf16[1,2048]{1,0:T(2,128)(2,1)S(1)}, bf16[1,2048]{1,0:T(2,128)(2,1)}, u32[]{:S(2)}) copy-start(bf16[1,2048]{1,0:T(2,128)(2,1)} %param.9) | copy-start | bytes 12292
  79.4 13.0 %copy-start.81 = (u32[32]{0:T(128)S(1)}, u32[32]{0:T(128)}, u32[]{:S(2)}) copy-start(u32[32]{0:T(128)} %constant.183) | copy-start | bytes 388
  79.4 16.1 %copy-start.16 = (bf16[2,64,2048]{2,1,0:T(8,128)(2,1)S(1)}, bf16[2,64,2048]{2,1,0:T(8,128)(2,1)}, u32[]{:S(2)}) copy-start(bf16[2,64,2048]{2,1,0:T(8,128)(2,1)} %param.7) | copy-start | bytes 1572868
  86.6 8.3 %collective-permute-start.1 = (bf16[64,2048]{1,0:T(8,128)(2,1)}, bf16[64,2048]{1,0:T(8,128)(2,1)S(1)}, u32[]{:S(2)}, u32[]{:S(2)}) collective-permute-start(bf16[64,2048]{1,0:T(8,128)(2,1)} %fusion.228), channel_id=1, source_target_pairs={{0,8},{8,16},{16,24},{1,9},{9,17},{17,25},{2,10},{10,18},{18,26},{... | collective-permute-start | bytes 786440 | tf_op jit(solution)/shard_map/ppermute | solution.py:16
  111.8 11.6 %copy-start.37 = (bf16[64,4,1,128]{3,2,1,0:T(2,128)(2,1)S(1)}, bf16[64,4,1,128]{3,2,1,0:T(2,128)(2,1)}, u32[]{:S(2)}) copy-start(bf16[64,4,1,128]{3,2,1,0:T(2,128)(2,1)} %get-tuple-element.83) | copy-start | bytes 196612
  134.4 11.9 %copy-start.56 = (f32[64]{0:T(128)S(1)}, f32[64]{0:T(128)}, u32[]{:S(2)}) copy-start(f32[64]{0:T(128)} %copy-done.55) | copy-start | bytes 772
  144.3 14.2 %copy-start.62 = (f32[4,4,64]{2,1,0:T(4,128)S(1)}, f32[4,4,64]{2,1,0:T(4,128)}, u32[]{:S(2)}) copy-start(f32[4,4,64]{2,1,0:T(4,128)} %get-tuple-element.109) | copy-start | bytes 12292
  145.0 6.7 collective-permute-start.2
  152.9 8.7 %collective-permute-start.3 = (bf16[64,2048]{1,0:T(8,128)(2,1)S(1)}, bf16[64,2048]{1,0:T(8,128)(2,1)S(1)}, u32[]{:S(2)}, u32[]{:S(2)}) collective-permute-start(bf16[64,2048]{1,0:T(8,128)(2,1)S(1)} %add_convert_fusion.2), channel_id=1, source_target_pairs={{0,8},{8,16},{16,24},{1,9},{9,17},{17,25},{2,10},{10,18},{18,26},{... | collective-permute-start | bytes 786440 | tf_op jit(solution)/shard_map/ppermute | solution.py:16
  179.2 11.6 %copy-start.38 = (bf16[64,4,1,128]{3,2,1,0:T(2,128)(2,1)S(1)}, bf16[64,4,1,128]{3,2,1,0:T(2,128)(2,1)}, u32[]{:S(2)}) copy-start(bf16[64,4,1,128]{3,2,1,0:T(2,128)(2,1)} %get-tuple-element.81) | copy-start | bytes 196612
  201.7 11.9 %copy-start.58 = (f32[64]{0:T(128)S(1)}, f32[64]{0:T(128)}, u32[]{:S(2)}) copy-start(f32[64]{0:T(128)} %copy-done.57) | copy-start | bytes 772
  211.6 13.8 %copy-start.63 = (f32[4,4,64]{2,1,0:T(4,128)S(1)}, f32[4,4,64]{2,1,0:T(4,128)}, u32[]{:S(2)}) copy-start(f32[4,4,64]{2,1,0:T(4,128)} %get-tuple-element.111) | copy-start | bytes 12292
  212.4 6.7 collective-permute-start.4
  220.3 8.3 %collective-permute-start.5 = (bf16[64,2048]{1,0:T(8,128)(2,1)S(1)}, bf16[64,2048]{1,0:T(8,128)(2,1)S(1)}, u32[]{:S(2)}, u32[]{:S(2)}) collective-permute-start(bf16[64,2048]{1,0:T(8,128)(2,1)S(1)} %add_convert_fusion.1), channel_id=1, source_target_pairs={{0,8},{8,16},{16,24},{1,9},{9,17},{17,25},{2,10},{10,18},{18,26},{... | collective-permute-start | bytes 786440 | tf_op jit(solution)/shard_map/ppermute | solution.py:16
  245.9 11.6 %copy-start.39 = (bf16[64,4,1,128]{3,2,1,0:T(2,128)(2,1)S(1)}, bf16[64,4,1,128]{3,2,1,0:T(2,128)(2,1)}, u32[]{:S(2)}) copy-start(bf16[64,4,1,128]{3,2,1,0:T(2,128)(2,1)} %get-tuple-element.79) | copy-start | bytes 196612
  268.5 11.9 %copy-start.60 = (f32[64]{0:T(128)S(1)}, f32[64]{0:T(128)}, u32[]{:S(2)}) copy-start(f32[64]{0:T(128)} %copy-done.59) | copy-start | bytes 772
  278.4 13.8 %copy-start.64 = (f32[4,4,64]{2,1,0:T(4,128)S(1)}, f32[4,4,64]{2,1,0:T(4,128)}, u32[]{:S(2)}) copy-start(f32[4,4,64]{2,1,0:T(4,128)} %get-tuple-element.113) | copy-start | bytes 12292
  279.1 6.7 collective-permute-start.6
  287.0 8.3 %collective-permute-start.7 = (bf16[64,2048]{1,0:T(8,128)(2,1)S(1)}, bf16[64,2048]{1,0:T(8,128)(2,1)S(1)}, u32[]{:S(2)}, u32[]{:S(2)}) collective-permute-start(bf16[64,2048]{1,0:T(8,128)(2,1)S(1)} %add_convert_fusion), channel_id=1, source_target_pairs={{0,8},{8,16},{16,24},{1,9},{9,17},{17,25},{2,10},{10,18},{18,26},{... | collective-permute-start | bytes 786440 | tf_op jit(solution)/shard_map/ppermute | solution.py:16
  338.0 12.1 %copy-start.25 = (bf16[5,64,2048]{2,1,0:T(8,128)(2,1)S(1)}, bf16[5,64,2048]{2,1,0:T(8,128)(2,1)}, u32[]{:S(2)}) copy-start(bf16[5,64,2048]{2,1,0:T(8,128)(2,1)} %get-tuple-element.135) | copy-start | bytes 3932164
  359.0 10.0 %copy-start.32 = (bf16[1,64,1024]{2,1,0:T(8,128)(2,1)S(1)}, bf16[1,64,1024]{2,1,0:T(8,128)(2,1)}, u32[]{:S(2)}) copy-start(bf16[1,64,1024]{2,1,0:T(8,128)(2,1)} %get-tuple-element.54) | copy-start | bytes 393220
  359.0 11.0 %copy-start.31 = (bf16[1,64,1024]{2,1,0:T(8,128)(2,1)S(1)}, bf16[1,64,1024]{2,1,0:T(8,128)(2,1)}, u32[]{:S(2)}) copy-start(bf16[1,64,1024]{2,1,0:T(8,128)(2,1)} %get-tuple-element.53) | copy-start | bytes 393220
  359.0 12.0 %copy-start.30 = (bf16[1,64,1024]{2,1,0:T(8,128)(2,1)S(1)}, bf16[1,64,1024]{2,1,0:T(8,128)(2,1)}, u32[]{:S(2)}) copy-start(bf16[1,64,1024]{2,1,0:T(8,128)(2,1)} %get-tuple-element.52) | copy-start | bytes 393220
  367.8 20.9 %collective-permute-start.11 = (bf16[64,2048]{1,0:T(8,128)(2,1)}, bf16[64,2048]{1,0:T(8,128)(2,1)S(1)}, u32[]{:S(2)}, u32[]{:S(2)}) collective-permute-start(bf16[64,2048]{1,0:T(8,128)(2,1)} %dynamic-slice_convert_fusion.4), channel_id=1, source_target_pairs={{0,4},{4,0},{1,5},{5,1},{2,6},{6,2},{3,7},{7,3},{8,12},{12,8},{9,1... | collective-permute-start | bytes 786440 | tf_op jit(solution)/shard_map/ppermute | solution.py:32
  374.7 14.0 %copy-start.7 = (bf16[2,64,2048]{2,1,0:T(8,128)(2,1)S(1)}, bf16[2,64,2048]{2,1,0:T(8,128)(2,1)}, u32[]{:S(2)}) copy-start(bf16[2,64,2048]{2,1,0:T(8,128)(2,1)} %param.13) | copy-start | bytes 1572868
  380.0 19.0 %copy-start.29 = (bf16[1,64,1024]{2,1,0:T(8,128)(2,1)S(1)}, bf16[1,64,1024]{2,1,0:T(8,128)(2,1)}, u32[]{:S(2)}) copy-start(bf16[1,64,1024]{2,1,0:T(8,128)(2,1)} %get-tuple-element.51) | copy-start | bytes 393220
  388.7 10.3 %copy-start.26 = (bf16[64,2048]{1,0:T(8,128)(2,1)}, bf16[64,2048]{1,0:T(8,128)(2,1)S(1)}, u32[]{:S(2)}) copy-start(bf16[64,2048]{1,0:T(8,128)(2,1)S(1)} %collective-permute-done.11) | copy-start | bytes 786436
  391.0 12.3 %collective-permute-start.12 = (bf16[64,2048]{1,0:T(8,128)(2,1)}, bf16[64,2048]{1,0:T(8,128)(2,1)}, u32[]{:S(2)}, u32[]{:S(2)}) collective-permute-start(bf16[64,2048]{1,0:T(8,128)(2,1)} %fusion.208), channel_id=1, source_target_pairs={{8,0},{16,8},{24,16},{9,1},{17,9},{25,17},{10,2},{18,10},{26,18},{... | collective-permute-start | bytes 786440 | tf_op jit(solution)/shard_map/ppermute | solution.py:16
  400.9 66.7 %collective-permute-start.21 = (bf16[128,2048]{1,0:T(8,128)(2,1)}, bf16[128,2048]{1,0:T(8,128)(2,1)}, u32[]{:S(2)}, u32[]{:S(2)}) collective-permute-start(bf16[128,2048]{1,0:T(8,128)(2,1)} %bitcast.761), channel_id=1, source_target_pairs={{0,2},{1,3},{2,0},{3,1},{4,6},{5,7},{6,4},{7,5},{8,10},{9,11},{10,... | collective-permute-start | bytes 1572872 | tf_op jit(solution)/shard_map/ppermute | solution.py:42
  412.9 15.9 %copy-start.36 = (bf16[64,4,1,128]{3,2,1,0:T(2,128)(2,1)S(1)}, bf16[64,4,1,128]{3,2,1,0:T(2,128)(2,1)}, u32[]{:S(2)}) copy-start(bf16[64,4,1,128]{3,2,1,0:T(2,128)(2,1)} %get-tuple-element.74) | copy-start | bytes 196612
  432.4 13.5 %copy-start.46 = (bf16[64,4,1,128]{3,0,1,2:T(8,128)(2,1)S(1)}, bf16[64,4,1,128]{3,0,1,2:T(8,128)(2,1)}, u32[]{:S(2)}) copy-start(bf16[64,4,1,128]{3,0,1,2:T(8,128)(2,1)} %fusion.150) | copy-start | bytes 196612
  456.6 7.2 %collective-permute-start.13 = (bf16[64,2048]{1,0:T(8,128)(2,1)}, bf16[64,2048]{1,0:T(8,128)(2,1)}, u32[]{:S(2)}, u32[]{:S(2)}) collective-permute-start(bf16[64,2048]{1,0:T(8,128)(2,1)} %dynamic-slice_convert_fusion.3), channel_id=1, source_target_pairs={{0,4},{4,0},{1,5},{5,1},{2,6},{6,2},{3,7},{7,3},{8,12},{12,8},{9,1... | collective-permute-start | bytes 786440 | tf_op jit(solution)/shard_map/ppermute | solution.py:32
  465.5 9.4 %collective-permute-start.14 = (bf16[64,2048]{1,0:T(8,128)(2,1)S(1)}, bf16[64,2048]{1,0:T(8,128)(2,1)S(1)}, u32[]{:S(2)}, u32[]{:S(2)}) collective-permute-start(bf16[64,2048]{1,0:T(8,128)(2,1)S(1)} %fusion.213), channel_id=1, source_target_pairs={{8,0},{16,8},{24,16},{9,1},{17,9},{25,17},{10,2},{18,10},{26,18},{... | collective-permute-start | bytes 786440 | tf_op jit(solution)/shard_map/ppermute | solution.py:16
  469.8 219.0 %collective-permute-start.22 = (bf16[256,2048]{1,0:T(8,128)(2,1)}, bf16[256,2048]{1,0:T(8,128)(2,1)}, u32[]{:S(2)}, u32[]{:S(2)}) collective-permute-start(bf16[256,2048]{1,0:T(8,128)(2,1)} %pad_maximum_fusion.3), channel_id=1, source_target_pairs={{0,1},{1,0},{2,3},{3,2},{4,5},{5,4},{6,7},{7,6},{8,9},{9,8},{10,11... | collective-permute-start | bytes 3145736 | tf_op jit(solution)/shard_map/ppermute | solution.py:42
  483.8 15.9 %copy-start.35 = (bf16[64,4,1,128]{3,2,1,0:T(2,128)(2,1)S(1)}, bf16[64,4,1,128]{3,2,1,0:T(2,128)(2,1)}, u32[]{:S(2)}) copy-start(bf16[64,4,1,128]{3,2,1,0:T(2,128)(2,1)} %get-tuple-element.72) | copy-start | bytes 196612
  503.4 13.6 %copy-start.47 = (bf16[64,4,1,128]{3,0,1,2:T(8,128)(2,1)S(1)}, bf16[64,4,1,128]{3,0,1,2:T(8,128)(2,1)}, u32[]{:S(2)}) copy-start(bf16[64,4,1,128]{3,0,1,2:T(8,128)(2,1)} %fusion.148) | copy-start | bytes 196612
  518.7 10.1 %copy-start.13 = (bf16[64,4096]{1,0:T(8,128)(2,1)S(1)}, bf16[64,4096]{1,0:T(8,128)(2,1)}, u32[]{:S(2)}) copy-start(bf16[64,4096]{1,0:T(8,128)(2,1)} %copy-done.12) | copy-start | bytes 1572868
  527.6 7.6 %collective-permute-start.15 = (bf16[64,2048]{1,0:T(8,128)(2,1)}, bf16[64,2048]{1,0:T(8,128)(2,1)}, u32[]{:S(2)}, u32[]{:S(2)}) collective-permute-start(bf16[64,2048]{1,0:T(8,128)(2,1)} %dynamic-slice_convert_fusion.2), channel_id=1, source_target_pairs={{0,4},{4,0},{1,5},{5,1},{2,6},{6,2},{3,7},{7,3},{8,12},{12,8},{9,1... | collective-permute-start | bytes 786440 | tf_op jit(solution)/shard_map/ppermute | solution.py:32
  536.9 8.3 %collective-permute-start.16 = (bf16[64,2048]{1,0:T(8,128)(2,1)S(1)}, bf16[64,2048]{1,0:T(8,128)(2,1)S(1)}, u32[]{:S(2)}, u32[]{:S(2)}) collective-permute-start(bf16[64,2048]{1,0:T(8,128)(2,1)S(1)} %fusion.218), channel_id=1, source_target_pairs={{8,0},{16,8},{24,16},{9,1},{17,9},{25,17},{10,2},{18,10},{26,18},{... | collective-permute-start | bytes 786440 | tf_op jit(solution)/shard_map/ppermute | solution.py:16
  553.9 15.9 %copy-start.34 = (bf16[64,4,1,128]{3,2,1,0:T(2,128)(2,1)S(1)}, bf16[64,4,1,128]{3,2,1,0:T(2,128)(2,1)}, u32[]{:S(2)}) copy-start(bf16[64,4,1,128]{3,2,1,0:T(2,128)(2,1)} %get-tuple-element.70) | copy-start | bytes 196612
  573.4 13.6 %copy-start.48 = (bf16[64,4,1,128]{3,0,1,2:T(8,128)(2,1)S(1)}, bf16[64,4,1,128]{3,0,1,2:T(8,128)(2,1)}, u32[]{:S(2)}) copy-start(bf16[64,4,1,128]{3,0,1,2:T(8,128)(2,1)} %fusion.146) | copy-start | bytes 196612
  595.9 12.8 %copy-start.65 = (f32[64]{0:T(128)S(1)}, f32[64]{0:T(128)}, u32[]{:S(2)}) copy-start(f32[64]{0:T(128)} %get-tuple-element.91) | copy-start | bytes 772
  595.9 12.8 %copy-start.66 = (f32[64]{0:T(128)S(1)}, f32[64]{0:T(128)}, u32[]{:S(2)}) copy-start(f32[64]{0:T(128)} %get-tuple-element.21) | copy-start | bytes 772
  595.9 12.8 %copy-start.67 = (f32[64]{0:T(128)S(1)}, f32[64]{0:T(128)}, u32[]{:S(2)}) copy-start(f32[64]{0:T(128)} %get-tuple-element.87) | copy-start | bytes 772
  595.9 12.8 %copy-start.68 = (f32[64]{0:T(128)S(1)}, f32[64]{0:T(128)}, u32[]{:S(2)}) copy-start(f32[64]{0:T(128)} %get-tuple-element.89) | copy-start | bytes 772
  597.7 7.2 %collective-permute-start.17 = (bf16[64,2048]{1,0:T(8,128)(2,1)}, bf16[64,2048]{1,0:T(8,128)(2,1)}, u32[]{:S(2)}, u32[]{:S(2)}) collective-permute-start(bf16[64,2048]{1,0:T(8,128)(2,1)} %dynamic-slice_convert_fusion.1), channel_id=1, source_target_pairs={{0,4},{4,0},{1,5},{5,1},{2,6},{6,2},{3,7},{7,3},{8,12},{12,8},{9,1... | collective-permute-start | bytes 786440 | tf_op jit(solution)/shard_map/ppermute | solution.py:32
  606.6 8.3 %collective-permute-start.18 = (bf16[64,2048]{1,0:T(8,128)(2,1)S(1)}, bf16[64,2048]{1,0:T(8,128)(2,1)S(1)}, u32[]{:S(2)}, u32[]{:S(2)}) collective-permute-start(bf16[64,2048]{1,0:T(8,128)(2,1)S(1)} %fusion.223), channel_id=1, source_target_pairs={{8,0},{16,8},{24,16},{9,1},{17,9},{25,17},{10,2},{18,10},{26,18},{... | collective-permute-start | bytes 786440 | tf_op jit(solution)/shard_map/ppermute | solution.py:16
  622.2 15.9 %copy-start.33 = (bf16[64,4,1,128]{3,2,1,0:T(2,128)(2,1)S(1)}, bf16[64,4,1,128]{3,2,1,0:T(2,128)(2,1)}, u32[]{:S(2)}) copy-start(bf16[64,4,1,128]{3,2,1,0:T(2,128)(2,1)} %get-tuple-element.68) | copy-start | bytes 196612
  641.6 13.5 %copy-start.45 = (bf16[64,4,1,128]{3,0,1,2:T(8,128)(2,1)S(1)}, bf16[64,4,1,128]{3,0,1,2:T(8,128)(2,1)}, u32[]{:S(2)}) copy-start(bf16[64,4,1,128]{3,0,1,2:T(8,128)(2,1)} %fusion.144) | copy-start | bytes 196612
  657.4 12.1 %collective-permute-start.19 = (bf16[128,3072]{1,0:T(8,128)(2,1)S(1)}, bf16[128,3072]{1,0:T(8,128)(2,1)S(1)}, u32[]{:S(2)}, u32[]{:S(2)}) collective-permute-start(bf16[128,3072]{1,0:T(8,128)(2,1)S(1)} %bitcast.754), channel_id=1, source_target_pairs={{0,2},{1,3},{2,0},{3,1},{4,6},{5,7},{6,4},{7,5},{8,10},{9,11},{10,... | collective-permute-start | bytes 2359304 | tf_op jit(solution)/shard_map/ppermute | solution.py:42
  664.1 8.6 %collective-permute-start.26 = (bf16[64,2048]{1,0:T(8,128)(2,1)S(1)}, bf16[64,2048]{1,0:T(8,128)(2,1)S(1)}, u32[]{:S(2)}, u32[]{:S(2)}) collective-permute-start(bf16[64,2048]{1,0:T(8,128)(2,1)S(1)} %dynamic-slice_convert_fusion), channel_id=1, source_target_pairs={{0,4},{4,0},{1,5},{5,1},{2,6},{6,2},{3,7},{7,3},{8,12},{12,8},{9,1... | collective-permute-start | bytes 786440 | tf_op jit(solution)/shard_map/ppermute | solution.py:32
  670.7 32.6 %collective-permute-start.20 = (bf16[256,3072]{1,0:T(8,128)(2,1)}, bf16[256,3072]{1,0:T(8,128)(2,1)}, u32[]{:S(2)}, u32[]{:S(2)}) collective-permute-start(bf16[256,3072]{1,0:T(8,128)(2,1)} %pad_maximum_fusion.1), channel_id=1, source_target_pairs={{0,1},{1,0},{2,3},{3,2},{4,5},{5,4},{6,7},{7,6},{8,9},{9,8},{10,11... | collective-permute-start | bytes 4718600 | tf_op jit(solution)/shard_map/ppermute | solution.py:42
  670.8 19.7 %copy-start.41 = (bf16[128,1024]{1,0:T(8,128)(2,1)S(1)}, bf16[128,1024]{1,0:T(8,128)(2,1)}, u32[]{:S(2)}) copy-start(bf16[128,1024]{1,0:T(8,128)(2,1)} %get-tuple-element.49) | copy-start | bytes 786436
  670.8 19.9 %copy-start.24 = (bf16[2,64,2048]{2,1,0:T(8,128)(2,1)S(1)}, bf16[2,64,2048]{2,1,0:T(8,128)(2,1)}, u32[]{:S(2)}) copy-start(bf16[2,64,2048]{2,1,0:T(8,128)(2,1)} %constant_dynamic-slice_fusion.6) | copy-start | bytes 1572868
  671.9 17.0 %collective-permute-start.23 = (bf16[128,1024]{1,0:T(8,128)(2,1)}, bf16[128,1024]{1,0:T(8,128)(2,1)S(1)}, u32[]{:S(2)}, u32[]{:S(2)}) collective-permute-start(bf16[128,1024]{1,0:T(8,128)(2,1)} %get-tuple-element.46), channel_id=1, source_target_pairs={{0,2},{1,3},{2,0},{3,1},{4,6},{5,7},{6,4},{7,5},{8,10},{9,11},{10,... | collective-permute-start | bytes 786440 | tf_op jit(solution)/shard_map/ppermute | solution.py:42
  672.4 18.0 %collective-permute-start.24 = (bf16[128,1024]{1,0:T(8,128)(2,1)}, bf16[128,1024]{1,0:T(8,128)(2,1)S(1)}, u32[]{:S(2)}, u32[]{:S(2)}) collective-permute-start(bf16[128,1024]{1,0:T(8,128)(2,1)} %get-tuple-element.45), channel_id=1, source_target_pairs={{0,1},{1,0},{2,3},{3,2},{4,5},{5,4},{6,7},{7,6},{8,9},{9,8},{10,11... | collective-permute-start | bytes 786440 | tf_op jit(solution)/shard_map/ppermute | solution.py:42
  672.7 18.1 %collective-permute-start.25 = (bf16[128,1024]{1,0:T(8,128)(2,1)}, bf16[128,1024]{1,0:T(8,128)(2,1)S(1)}, u32[]{:S(2)}, u32[]{:S(2)}) collective-permute-start(bf16[128,1024]{1,0:T(8,128)(2,1)} %get-tuple-element.44), channel_id=1, source_target_pairs={{0,3},{1,2},{2,1},{3,0},{4,7},{5,6},{6,5},{7,4},{8,11},{9,10},{10,... | collective-permute-start | bytes 786440 | tf_op jit(solution)/shard_map/ppermute | solution.py:42
  688.9 9.1 %collective-permute-start.10 = (bf16[128,1024]{1,0:T(8,128)(2,1)}, bf16[128,1024]{1,0:T(8,128)(2,1)S(1)}, u32[]{:S(2)}, u32[]{:S(2)}) collective-permute-start(bf16[128,1024]{1,0:T(8,128)(2,1)} %get-tuple-element.48), channel_id=1, source_target_pairs={{0,3},{1,2},{2,1},{3,0},{4,7},{5,6},{6,5},{7,4},{8,11},{9,10},{10,... | collective-permute-start | bytes 786440 | tf_op jit(solution)/shard_map/ppermute | solution.py:42
  688.9 14.4 %collective-permute-start.8 = (bf16[128,1024]{1,0:T(8,128)(2,1)}, bf16[128,1024]{1,0:T(8,128)(2,1)S(1)}, u32[]{:S(2)}, u32[]{:S(2)}) collective-permute-start(bf16[128,1024]{1,0:T(8,128)(2,1)} %get-tuple-element.50), channel_id=1, source_target_pairs={{0,2},{1,3},{2,0},{3,1},{4,6},{5,7},{6,4},{7,5},{8,10},{9,11},{10,... | collective-permute-start | bytes 786440 | tf_op jit(solution)/shard_map/ppermute | solution.py:42
  690.5 12.8 %collective-permute-start.9 = (bf16[128,1024]{1,0:T(8,128)(2,1)S(1)}, bf16[128,1024]{1,0:T(8,128)(2,1)S(1)}, u32[]{:S(2)}, u32[]{:S(2)}) collective-permute-start(bf16[128,1024]{1,0:T(8,128)(2,1)S(1)} %copy-done.41), channel_id=1, source_target_pairs={{0,1},{1,0},{2,3},{3,2},{4,5},{5,4},{6,7},{7,6},{8,9},{9,8},{10,11... | collective-permute-start | bytes 786440 | tf_op jit(solution)/shard_map/ppermute | solution.py:42
  690.7 12.6 %copy-start.40 = (bf16[128,1024]{1,0:T(8,128)(2,1)S(1)}, bf16[128,1024]{1,0:T(8,128)(2,1)}, u32[]{:S(2)}) copy-start(bf16[128,1024]{1,0:T(8,128)(2,1)} %get-tuple-element.47) | copy-start | bytes 786436
  698.0 9.9 %copy-start.75 = (bf16[128,1024]{1,0:T(8,128)(2,1)}, bf16[128,1024]{1,0:T(8,128)(2,1)S(1)}, u32[]{:S(2)}) copy-start(bf16[128,1024]{1,0:T(8,128)(2,1)S(1)} %collective-permute-done.10) | copy-start | bytes 786436
  (45 other events, 161.6 us)

commit v2 on v1

v2 whole, which is shorter than its diff:
```python
import functools

import jax
import jax.numpy as jnp
from jax import lax
from jax.experimental import pallas as pl
from jax.experimental.pallas import tpu as pltpu
from jax.sharding import PartitionSpec as P

HEAD_DIM = 128


EPS = 1e-05
NEG = -1e30


def inner(former, latter):
    return lax.dot_general(
        former, latter, (((0,), (0,)), ((), ())), preferred_element_type=jnp.float32
    )


def outer_side(former, latter):
    return lax.dot_general(
        former, latter, (((1,), (1,)), ((), ())), preferred_element_type=jnp.float32
    )


def plain(former, latter):
    return jnp.dot(former, latter, preferred_element_type=jnp.float32)


def replica_bits():
    ranks = lax.axis_size("dp")
    return [1 << power for power in reversed(range(ranks.bit_length() - 1))]


def exchange(block, mask):
    return lax.ppermute(block, "dp", [(i, i ^ mask) for i in range(lax.axis_size("dp"))])


def every_row(block):
    for bit in replica_bits():
        block = jnp.concatenate([block, exchange(block, bit)], 0)
    return block


def own_columns(block):
    ranks = lax.axis_size("dp")
    rank = lax.axis_index("dp")
    width = block.shape[1] // ranks
    masks = [0]
    for bit in replica_bits():
        masks = masks + [mask ^ bit for mask in masks]
    pieces = []
    for mask in masks:
        target = jnp.bitwise_xor(rank, mask)
        piece = lax.dynamic_slice_in_dim(block, target * width, width, 1)
        pieces.append(exchange(piece, mask) if mask else piece)
    return jnp.concatenate(pieces, 0)


def tile_of(width):
    return 512 if width % 512 == 0 else 256


def tiles(width, body):
    size = tile_of(width)

    def step(index, carry):
        body(pl.multiple_of(index * size, size), size)
        return carry

    lax.fori_loop(0, width // size, step, 0)


def kernel(
    ranks, sections, micro,
    hidden, mask, gains, wq_hbm, wkv_hbm, wo_hbm, grad_out,
    normed, mixed, pair_rows, grad_rows, gain_grad,
    wq, wkv, wo, hfull, gfull, gain_all, scales, queries, keyval, weights, mix_grad,
    own, send_f, recv_f, send_b, recv_b, next_h, next_g, corr_out, corr_in,
    load_sem, gain_sem, ag_sem, rs_sem, z_sem, corr_sem,
):
    rank = lax.axis_index("tensor")
    station = lax.axis_index("section")
    rows = hidden.shape[1]
    width = hidden.shape[2]
    model = ranks * width
    q_width = wq.shape[1]
    pairs = wkv.shape[1] // (2 * HEAD_DIM)
    group = q_width // (HEAD_DIM * pairs)
    first, last = station == 0, station == sections - 1

    def peer(distance):
        return lax.rem(rank + distance, ranks)

    def remote(source, target, sems, device):
        return pltpu.make_async_remote_copy(
            src_ref=source, dst_ref=target, send_sem=sems[0], recv_sem=sems[1],
            device_id=device, device_id_type=pl.DeviceIdType.MESH,
        )

    barrier = pltpu.get_barrier_semaphore()
    for distance in range(1, ranks):
        pl.semaphore_signal(
            barrier, inc=1, device_id={"tensor": peer(distance)},
            device_id_type=pl.DeviceIdType.MESH,
        )

    @pl.when(station > 0)
    def _():
        pl.semaphore_signal(
            barrier, inc=1, device_id={"section": station - 1},
            device_id_type=pl.DeviceIdType.MESH,
        )

    @pl.when(station < sections - 1)
    def _():
        pl.semaphore_signal(
            barrier, inc=1, device_id={"section": station + 1},
            device_id_type=pl.DeviceIdType.MESH,
        )

    loads = [
        pltpu.make_async_copy(source, target, load_sem.at[index])
        for index, (source, target) in enumerate(((wq_hbm, wq), (wkv_hbm, wkv), (wo_hbm, wo)))
    ]
    for load in loads:
        load.start()

    ends = jnp.where(first, 0, 1) + jnp.where(last, 0, 1)
    pl.semaphore_wait(barrier, ranks - 1 + ends)

    def gain_copy(distance):
        return remote(
            gain_all.at[rank], gain_all.at[rank],
            (gain_sem.at[0, distance - 1], gain_sem.at[1, distance - 1]),
            {"tensor": peer(distance)},
        )

    def gather_copy(way, m, distance):
        full = (hfull, gfull)[way]
        return remote(
            full.at[m, rank], full.at[m, rank],
            (ag_sem.at[way, 0, m, distance - 1], ag_sem.at[way, 1, m, distance - 1]),
            {"tensor": peer(distance)},
        )

    def sum_copy(way, m, distance):
        return remote(
            (send_f, send_b)[way].at[m, distance - 1], (recv_f, recv_b)[way].at[m, distance - 1],
            (rs_sem.at[way, 0, m, distance - 1], rs_sem.at[way, 1, m, distance - 1]),
            {"tensor": peer(distance)},
        )

    def corr_copy(m, distance):
        return remote(
            corr_out.at[m], corr_in.at[m, distance - 1],
            (corr_sem.at[0, m, distance - 1], corr_sem.at[1, m, distance - 1]),
            {"tensor": peer(distance)},
        )

    def hop_copy(way, m):
        target = station + 1 if way == 0 else station - 1
        target = lax.rem(target + sections, sections)
        return remote(
            (next_h, next_g)[way].at[m], (hfull, gfull)[way].at[m, rank],
            (z_sem.at[way, 0, m], z_sem.at[way, 1, m]),
            {"section": target},
        )

    def spread(way, m):
        for distance in range(1, ranks):
            gather_copy(way, m, distance).start()

    gain_all[rank] = gains[...]
    for distance in range(1, ranks):
        gain_copy(distance).start()

    @pl.when(first)
    def _():
        for m in range(micro):
            hfull[m, rank] = hidden[m]
            spread(0, m)

    @pl.when(last)
    def _():
        for m in range(micro):
            gfull[m, rank] = grad_out[m]
            spread(1, m)

    for distance in range(1, ranks):
        gain_copy(distance).wait()

    def gather(way, m, at_source):
        @pl.when(jnp.logical_not(at_source))
        def _():
            hop_copy(way, m).wait_recv()
            spread(way, m)

        for distance in range(1, ranks):
            gather_copy(way, m, distance).wait()

    def gain_of(owner):
        return gain_all[owner][:1].astype(jnp.float32)

    def stack(block):
        return jnp.concatenate(
            [block[:, a * HEAD_DIM:(a + 1) * HEAD_DIM] for a in range(group)], 0
        )

    def head_parts(m, g):
        query = stack(queries[m, :, g * group * HEAD_DIM:(g + 1) * group * HEAD_DIM])
        key = keyval[m, :, 2 * g * HEAD_DIM:(2 * g + 1) * HEAD_DIM]
        value = keyval[m, :, (2 * g + 1) * HEAD_DIM:(2 * g + 2) * HEAD_DIM]
        return query, key, value

    def forward(m, carry):
        gather(0, m, first)
        line = pl.ds(pl.multiple_of(m * rows, rows), rows)
        total = jnp.zeros((rows, 1), jnp.float32)
        for owner in range(ranks):
            wide = hfull[m, owner].astype(jnp.float32)
            total = total + jnp.sum(wide * wide, -1, keepdims=True)
        scale = lax.rsqrt(total / model + EPS)
        scales[m] = jnp.broadcast_to(scale, (rows, HEAD_DIM))
        for owner in range(ranks):
            wide = hfull[m, owner].astype(jnp.float32)
            normed[line, owner * width:(owner + 1) * width] = (
                wide * scale * gain_of(owner)
            ).astype(jnp.bfloat16)

        @pl.when(m == 0)
        def _():
            loads[0].wait()
            loads[1].wait()

        def project_q(start, size):
            columns = pl.ds(start, size)
            queries[m, :, columns] = plain(normed[line, :], wq[:, columns]).astype(jnp.bfloat16)

        def project_kv(start, size):
            columns = pl.ds(start, size)
            keyval[m, :, columns] = plain(normed[line, :], wkv[:, columns]).astype(jnp.bfloat16)

        tiles(q_width, project_q)
        tiles(wkv.shape[1], project_kv)
        allowed = jnp.concatenate([mask[m]] * group, 0) > 0.5
        for g in range(pairs):
            query, key, value = head_parts(m, g)
            scores = outer_side(query, key) * HEAD_DIM ** (-0.5)
            scores = jnp.where(allowed, scores, NEG)
            raised = jnp.exp(scores - jnp.max(scores, -1, keepdims=True))
            attn = raised / jnp.sum(raised, -1, keepdims=True)
            weights[m, g] = attn
            mix = plain(attn.astype(jnp.bfloat16), value).astype(jnp.bfloat16)
            for a in range(group):
                at = (g * group + a) * HEAD_DIM
                mixed[line, at:at + HEAD_DIM] = mix[a * rows:(a + 1) * rows]

        @pl.when(m == 0)
        def _():
            loads[2].wait()

        @pl.when(jnp.logical_not(last))
        def _():
            for distance in range(1, ranks):
                base = peer(distance) * width

                def project_far(start, size):
                    far = pl.ds(pl.multiple_of(base + start, size), size)
                    send_f[m, distance - 1, :, pl.ds(start, size)] = plain(
                        mixed[line, :], wo[:, far]
                    ).astype(jnp.bfloat16)

                tiles(width, project_far)
                sum_copy(0, m, distance).start()

            def project_own(start, size):
                near = pl.ds(pl.multiple_of(rank * width + start, size), size)
                own[:, pl.ds(start, size)] = plain(mixed[line, :], wo[:, near])

            tiles(width, project_own)
            result = own[...]
            for distance in range(1, ranks):
                sum_copy(0, m, distance).wait()
                result = result + recv_f[m, distance - 1].astype(jnp.float32)
            next_h[m] = (hfull[m, rank].astype(jnp.float32) + result).astype(jnp.bfloat16)
            hop_copy(0, m).start()

        return carry

    lax.fori_loop(0, micro, forward, 0)
    gain_grad[...] = jnp.zeros(gain_grad.shape, jnp.float32)

    def backward(m, carry):
        gather(1, m, last)
        line = pl.ds(pl.multiple_of(m * rows, rows), rows)
        for owner in range(ranks):
            grad_rows[line, owner * width:(owner + 1) * width] = gfull[m, owner]

        def back_out(start, size):
            part = pl.ds(start, size)
            mix_grad[:, part] = outer_side(grad_rows[line, :], wo[part, :]).astype(jnp.bfloat16)

        tiles(q_width, back_out)
        for g in range(pairs):
            query, key, value = head_parts(m, g)
            attn = weights[m, g]
            grads = stack(mix_grad[:, g * group * HEAD_DIM:(g + 1) * group * HEAD_DIM])
            value_grad = inner(attn.astype(jnp.bfloat16), grads).astype(jnp.bfloat16)
            weight_grad = outer_side(grads, value)
            score_grad = (
                attn
                * (weight_grad - jnp.sum(weight_grad * attn, -1, keepdims=True))
                * HEAD_DIM ** (-0.5)
            ).astype(jnp.bfloat16)
            query_grad = plain(score_grad, key).astype(jnp.bfloat16)
            key_grad = inner(score_grad, query).astype(jnp.bfloat16)
            for a in range(group):
                at = (g * group + a) * HEAD_DIM
                pair_rows[line, at:at + HEAD_DIM] = query_grad[a * rows:(a + 1) * rows]
            at = q_width + 2 * g * HEAD_DIM
            pair_rows[line, at:at + HEAD_DIM] = key_grad
            pair_rows[line, at + HEAD_DIM:at + 2 * HEAD_DIM] = value_grad

        def back_in(base, start, size):
            part = pl.ds(pl.multiple_of(base + start, size), size)
            return outer_side(pair_rows[line, :q_width], wq[part, :]) + outer_side(
                pair_rows[line, q_width:], wkv[part, :]
            )

        corr_out[m] = jnp.zeros((rows, HEAD_DIM), jnp.float32)

        def correct(partial, owner, start, size):
            columns = pl.ds(start, size)
            gain = gain_all[owner, :, columns][:1].astype(jnp.float32)
            wide = hfull[m, owner, :, columns].astype(jnp.float32)
            corr_out[m] += jnp.broadcast_to(
                jnp.sum(partial * gain * wide, -1, keepdims=True), (rows, HEAD_DIM)
            )

        for distance in range(1, ranks):
            owner = peer(distance)

            def far(start, size):
                partial = back_in(owner * width, start, size)
                correct(partial, owner, start, size)
                send_b[m, distance - 1, :, pl.ds(start, size)] = partial.astype(jnp.bfloat16)

            tiles(width, far)
            sum_copy(1, m, distance).start()

        def near(start, size):
            partial = back_in(rank * width, start, size)
            correct(partial, rank, start, size)
            own[:, pl.ds(start, size)] = partial

        tiles(width, near)
        for distance in range(1, ranks):
            corr_copy(m, distance).start()
        normed_grad = own[...]
        for distance in range(1, ranks):
            sum_copy(1, m, distance).wait()
            normed_grad = normed_grad + recv_b[m, distance - 1].astype(jnp.float32)
        own[...] = normed_grad
        scale = scales[m][:, :1]
        wide = hfull[m, rank].astype(jnp.float32)
        gain_grad[...] += jnp.sum(own[...] * wide * scale, 0, keepdims=True)
        for distance in range(1, ranks):
            corr_copy(m, distance).wait()

        @pl.when(station > 0)
        def _():
            correction = corr_out[m]
            for distance in range(1, ranks):
                correction = correction + corr_in[m, distance - 1]
            factor = scale * scale * scale / model * correction[:, :1]
            next_g[m] = (
                gfull[m, rank].astype(jnp.float32)
                + scale * gain_of(rank) * own[...]
                - hfull[m, rank].astype(jnp.float32) * factor
            ).astype(jnp.bfloat16)
            hop_copy(1, m).start()

        return carry

    lax.fori_loop(0, micro, backward, 0)

    @pl.when(jnp.logical_not(last))
    def _():
        for m in range(micro):
            hop_copy(0, m).wait_send()

    @pl.when(station > 0)
    def _():
        for m in range(micro):
            hop_copy(1, m).wait_send()


def layers(hidden_in, mask, gains, query_weight, pair_weight, out_weight, grad_out):
    ranks, sections = lax.axis_size("tensor"), lax.axis_size("section")
    micro, rows, width = hidden_in.shape
    model = ranks * width
    q_width, kv_width = query_weight.shape[1], pair_weight.shape[1]
    pairs = kv_width // (2 * HEAD_DIM)
    group = q_width // (HEAD_DIM * pairs)
    half, wide = jnp.bfloat16, jnp.float32
    vmem = pl.BlockSpec(memory_space=pltpu.VMEM)
    anywhere = pl.BlockSpec(memory_space=pl.ANY)
    others = ranks - 1
    return pl.pallas_call(
        functools.partial(kernel, ranks, sections, micro),
        out_shape=(
            jax.ShapeDtypeStruct((micro * rows, model), half),
            jax.ShapeDtypeStruct((micro * rows, q_width), half),
            jax.ShapeDtypeStruct((micro * rows, q_width + kv_width), half),
            jax.ShapeDtypeStruct((micro * rows, model), half),
            jax.ShapeDtypeStruct((1, width), wide),
        ),
        in_specs=[vmem, vmem, vmem, anywhere, anywhere, anywhere, vmem],
        out_specs=(vmem,) * 5,
        scratch_shapes=[
            pltpu.VMEM((model, q_width), half),
            pltpu.VMEM((model, kv_width), half),
            pltpu.VMEM((q_width, model), half),
            pltpu.VMEM((micro, ranks, rows, width), half),
            pltpu.VMEM((micro, ranks, rows, width), half),
            pltpu.VMEM((ranks, 16, width), half),
            pltpu.VMEM((micro, rows, HEAD_DIM), wide),
            pltpu.VMEM((micro, rows, q_width), half),
            pltpu.VMEM((micro, rows, kv_width), half),
            pltpu.VMEM((micro, pairs, group * rows, rows), wide),
            pltpu.VMEM((rows, q_width), half),
            pltpu.VMEM((rows, width), wide),
            pltpu.VMEM((micro, others, rows, width), half),
            pltpu.VMEM((micro, others, rows, width), half),
            pltpu.VMEM((micro, others, rows, width), half),
            pltpu.VMEM((micro, others, rows, width), half),
            pltpu.VMEM((micro, rows, width), half),
            pltpu.VMEM((micro, rows, width), half),
            pltpu.VMEM((micro, rows, HEAD_DIM), wide),
            pltpu.VMEM((micro, others, rows, HEAD_DIM), wide),
            pltpu.SemaphoreType.DMA((3,)),
            pltpu.SemaphoreType.DMA((2, others)),
            pltpu.SemaphoreType.DMA((2, 2, micro, others)),
            pltpu.SemaphoreType.DMA((2, 2, micro, others)),
            pltpu.SemaphoreType.DMA((2, 2, micro)),
            pltpu.SemaphoreType.DMA((2, micro, others)),
        ],
        compiler_params=pltpu.CompilerParams(
            collective_id=0, has_side_effects=True, vmem_limit_bytes=60 << 20
        ),
    )(hidden_in, mask, gains, query_weight, pair_weight, out_weight, grad_out)


def shards(hidden_in, lengths, gains, w_query, w_keyval, w_out, grad_out):
    row_count = hidden_in.shape[1]
    query_weight = w_query[0]
    model_width = query_weight.shape[0]
    pair_count = w_keyval.shape[2]
    pair_weight = w_keyval[0].reshape(model_width, -1)
    position = jnp.arange(row_count)
    causal = position[None, :] <= position[:, None]
    mask = (causal[None] & (position[None, None, :] < lengths[:, None, None])).astype(jnp.float32)
    gain_rows = jnp.broadcast_to(gains, (16, gains.shape[1]))
    normed_rows, mixed_rows, pair_rows, outgrad_rows, gain_grad = layers(
        hidden_in, mask, gain_rows, query_weight, pair_weight, w_out[0], grad_out
    )
    mixed_rows = every_row(mixed_rows)
    output_total = inner(mixed_rows, own_columns(outgrad_rows))
    normed_rows = own_columns(normed_rows)
    pair_rows = every_row(pair_rows)
    query_width = query_weight.shape[1]
    query_total = inner(normed_rows, pair_rows[:, :query_width])
    pair_total = inner(normed_rows, pair_rows[:, query_width:])
    gain_total = lax.psum_scatter(gain_grad[0], "dp", scatter_dimension=0, tiled=True)
    grad_query = query_total[None]
    grad_keyval = pair_total.reshape(1, pair_total.shape[0], pair_count, 2 * HEAD_DIM)
    grad_outproj = output_total[None]
    grad_gain = gain_total[None]
    return (grad_query, grad_keyval, grad_outproj, grad_gain)


def solution(mesh):
    in_specs = (
        P("dp", None, "tensor"),
        P("dp"),
        P("section", "tensor"),
        P("section", None, "tensor"),
        P("section", None, "tensor", None),
        P("section", "tensor", None),
        P("dp", None, "tensor"),
    )
    out_specs = (
        P("section", "dp", "tensor"),
        P("section", "dp", "tensor", None),
        P("section", "tensor", "dp"),
        P("section", ("tensor", "dp")),
    )
    return jax.shard_map(shards, mesh=mesh, in_specs=in_specs, out_specs=out_specs, check_vma=False)
```

time: 732 us -> 336 us (0.46); the launches traced: 721 us -> 336 us
  matrix products: 343 us -> 17.9 us
  Pallas kernels: 0 us -> 254 us
  blocking collectives: 117 us -> 14 us
  local copies, waits for them, and re-layouts: 122 us -> 20.4 us
  other arithmetic: 57.6 us -> 4.88 us
  starting transfers between devices: 39.3 us -> 6.43 us
  waiting for transfers between devices: 39.3 us -> 16.3 us
    dot_general x59 -> x0, matrix products: 313 us -> none  [the longest x15 149 us: outer_side(): lax.dot_general(former, latter, (((1,), (1,)), ((), ())), preferred_eleme...]
    pallas_call x0 -> x1, Pallas kernels: none -> 254 us  [layers(): pl.pallas_call(functools.partial(kernel, ranks, sections, micro), out_sha...]
    all_gather x11 -> x0, blocking collectives: 81.8 us -> none  [features(): return lax.all_gather(operand, 'tensor', axis=1, tiled=True)]
    ppermute x17 -> x0, starting transfers between devices: 33.2 us -> none  [the longest x8 22.4 us: shifted(): return lax.ppermute(block, axis, route)]
    convert_element_type x33 -> x0, local copies, waits for them, and re-layouts: 31.6 us -> none  [the longest x14 15.4 us: attend(): return (head_mix.reshape(row_count, -1).astype(jnp.bfloat16), attn_weights)]
    ppermute x17 -> x0, waiting for transfers between devices: 29.9 us -> none  [the longest x8 20.4 us: shifted(): return lax.ppermute(block, axis, route)]
    reshape x30 -> x0, local copies, waits for them, and re-layouts: 28.5 us -> none  [the longest x5 9.13 us: attend_back(): query_heads = queries.reshape(row_count, pair_count, group_size, HEAD_DIM)]
    psum x4 -> x0, blocking collectives: 22.1 us -> none  [shards(): lax.psum(jnp.sum(partial_grad * gain_full * current_full, -1), 'tensor')]
  transfers between devices with their start and end apart: 27 -> 10, of which waited for: 11 -> 3; matrix products, arithmetic and copies ran while one was open for 35% -> 5% of each run, Pallas kernels for 0% -> 0%
where the time goes in v2:
time: 336 us
  Pallas kernels  254 us (76%)
  local copies, waits for them, and re-layouts  20.4 us (6%)
  matrix products  17.9 us (5%)
  waiting for transfers between devices  16.3 us (5%)
  blocking collectives  14 us (4%)
  starting transfers between devices  6.43 us (2%)
  other arithmetic  4.88 us (1%)
    pallas_call x1, Pallas kernels, layers(): pl.pallas_call(functools.partial(kernel, ranks, sections, micro), out_sha...  254 us
    dot_general x3, matrix products, inner(): lax.dot_general(former, latter, (((0,), (0,)), ((), ())), preferred_eleme...  17.9 us
    ppermute x10, waiting for transfers between devices, exchange(): lax.ppermute(block, 'dp', [(i, i ^ mask) for i in range(lax.axis_size('dp...  16.3 us
    unnamed x28, local copies, waits for them, and re-layouts  16.2 us
    unnamed x1, blocking collectives  14 us
  transfers between devices with their start and end apart: 10, of which 3 were waited for; matrix products, arithmetic and copies ran while one was open for 5% of the time, Pallas kernels for 0%

profile of v2, /device:TPU:0, one launch (start us, length us, event | category | flops | bytes accessed | tf_op | source)
XLA Modules:
  0.0 335.6 jit_solution(17600648461671605363)
XLA Ops:
  0.6 0.7 iota_compare_fusion.1
  1.4 0.0 copy-start.8
  1.4 9.5 %copy.13 = bf16[512,8,4,256]{3,1,2,0:T(8,128)(2,1)} copy(bf16[512,8,4,256]{3,2,1,0:T(4,128)(2,1)} %bitcast.16) | data formatting | bytes 16777216
  10.9 0.0 copy-done.8
  11.0 0.6 and_convert_fusion.mask
  11.6 0.6 broadcast_in_dim.22.gains
  12.2 254.3 %shard_map.102 = (bf16[128,4096]{1,0:T(8,128)(2,1)}, bf16[128,2048]{1,0:T(8,128)(2,1)}, bf16[128,3072]{1,0:T(8,128)(2,1)}, bf16[128,4096]{1,0:T(8,128)(2,1)}, f32[1,2048]{1,0:T(1,128)}) custom-call(bf16[2,64,2048]{2,1,0:T(8,128)(2,1)} %hidden.1, f32[2,64,64]{2,1,0:T(8,128)} %and_convert_fusion.mask, bf16[16,2048]{1,0:T(8,128)(2,1)} %broadcast_in_dim.22.gains, ...), custom_call_target="tpu_custom_call" | custom-call | tf_op jit(solution)/shard_map/pallas_call | solution.py:413
  266.5 0.0 copy-start.1
  266.5 1.6 collective-permute-start.3
  268.1 0.5 collective-permute-start.5
  268.6 10.2 %collective-permute-done.3 = bf16[128,3072]{1,0:T(8,128)(2,1)S(1)} collective-permute-done((bf16[128,3072]{1,0:T(8,128)(2,1)}, bf16[128,3072]{1,0:T(8,128)(2,1)S(1)}, u32[]{:S(2)}, u32[]{:S(2)}) %collective-permute-start.3) | collective-permute-done | bytes 786464 | tf_op jit(solution)/shard_map/ppermute | solution.py:39
  278.8 2.4 pad_maximum_fusion
  281.2 0.0 copy-start.10
  281.2 0.0 copy-start.9
  281.2 0.0 collective-permute-start.4
  281.2 3.2 collective-permute-done.5
  284.4 0.0 copy-done.1
  284.4 0.0 copy-start.3
  284.4 1.1 pad_maximum_fusion.2
  285.5 0.0 copy-done.3
  285.5 0.0 collective-permute-start.6
  285.6 0.0 copy-start
  285.6 2.2 constant_dynamic-slice_fusion.3
  287.7 1.6 collective-permute-start.9
  289.4 0.0 collective-permute-start.8
  289.4 0.5 collective-permute-start.7
  289.9 0.0 copy-done.10
  289.9 0.6 dynamic-slice
  291.1 0.0 copy-done.9
  291.1 14.0 %all-reduce = f32[2048]{0:T(1024)S(1)} all-reduce(f32[2048]{0:T(1024)S(1)} %bitcast.18), channel_id=2, replica_groups=mesh['section'=4,'tensor'=2,'dp'=4] {'dp'}, use_global_device_ids=true, to_apply=%region_0.0.clone | all-reduce | flops 2048 | bytes 16384
  305.2 0.7 dynamic-slice.1
  305.8 1.3 constant_dynamic-slice_fusion.7
  307.1 0.0 copy-done
  307.1 0.0 copy-start.5
  307.1 0.0 copy-start.2
  307.1 0.0 copy-start.4
  307.1 0.1 constant_dynamic-update-slice_fusion.2
  307.2 0.1 constant_dynamic-update-slice_fusion.1
  307.2 0.0 collective-permute-done.9
  307.3 0.1 collective-permute-start.2
  307.3 0.0 collective-permute-done.8
  307.3 0.6 collective-permute-start.1
  307.9 0.0 collective-permute-done.7
  308.0 1.5 collective-permute-start
  309.5 0.0 collective-permute-done.6
  309.5 0.0 copy-done.2
  309.5 0.0 copy-done.4
  309.5 7.2 %convolution_bitcast_fusion = f32[1,2048,1024]{2,1,0:T(8,128)} fusion(bf16[256,2048]{1,0:T(8,128)(2,1)} %collective-permute-done.6, bf16[128,2048]{1,0:T(8,128)(2,1)S(1)} %copy-done.4, bf16[128,2048]{1,0:T(8,128)(2,1)S(1)} %copy-done.2, bf16[128,1024]{1,0:T(8,128)(2,1)} %collective-permute-done.9, bf16[128,1024]{1,0:T(8,128)(2,1)} %collective-permute-done.8, ...), kind=kOutput, calls=%fused_computation | convolution fusion | flops 2157969408 | bytes 11534336 | tf_op jit(solution)/shard_map/dot_general | solution.py:18
  316.7 0.0 collective-permute-done.4
  316.7 0.1 constant_dynamic-update-slice_fusion
  316.8 0.0 copy-start.7
  316.8 0.0 collective-permute-done.2
  316.8 0.0 collective-permute-done.1
  316.8 2.9 collective-permute-done
  319.7 0.0 copy-done.5
  319.7 3.3 fusion.6
  323.0 0.0 copy-done.7
  323.0 0.0 copy-start.6
  323.0 5.3 %copy.12 = f32[1,1024,4,256]{3,2,1,0:T(4,128)} copy(f32[1,1024,4,256]{1,3,2,0:T(8,128)} %bitcast.17) | data formatting | bytes 8388608
  328.3 0.0 copy-done.6
  328.3 7.4 %convolution_bitcast_fusion.1 = f32[1,1024,2048]{2,1,0:T(8,128)} fusion(bf16[512,3072]{1,0:T(8,128)(2,1)} %copy-done.7, bf16[128,1024]{1,0:T(8,128)(2,1)S(1)} %collective-permute-done.2, bf16[128,1024]{1,0:T(8,128)(2,1)S(1)} %collective-permute-done.1, bf16[128,1024]{1,0:T(8,128)(2,1)S(1)} %collective-permute-done, bf16[128,1024]{1,0:T(8,128)(2,1)S(1)} %copy-done.6), kind=kOutput, calls=%fused_computation.1 | convolution fusion | flops 2151677952 | bytes 11534336 | tf_op jit(solution)/shard_map/dot_general | solution.py:18
  (2 shorter events, 0.0 us)
Async XLA Ops:
  1.4 9.5 %copy-start.8 = (bf16[1,2048]{1,0:T(2,128)(2,1)S(1)}, bf16[1,2048]{1,0:T(2,128)(2,1)}, u32[]{:S(2)}) copy-start(bf16[1,2048]{1,0:T(2,128)(2,1)} %param.9) | copy-start | bytes 12292
  266.5 17.9 %copy-start.1 = (bf16[128,2048]{1,0:T(8,128)(2,1)S(1)}, bf16[128,2048]{1,0:T(8,128)(2,1)}, u32[]{:S(2)}) copy-start(bf16[128,2048]{1,0:T(8,128)(2,1)} %get-tuple-element.11) | copy-start | bytes 1572868
  266.5 12.3 %collective-permute-start.3 = (bf16[128,3072]{1,0:T(8,128)(2,1)}, bf16[128,3072]{1,0:T(8,128)(2,1)S(1)}, u32[]{:S(2)}, u32[]{:S(2)}) collective-permute-start(bf16[128,3072]{1,0:T(8,128)(2,1)} %get-tuple-element.10), channel_id=1, source_target_pairs={{0,2},{1,3},{2,0},{3,1},{4,6},{5,7},{6,4},{7,5},{8,10},{9,11},{10,... | collective-permute-start | bytes 2359304 | tf_op jit(solution)/shard_map/ppermute | solution.py:39
  268.1 16.3 %collective-permute-start.5 = (bf16[128,2048]{1,0:T(8,128)(2,1)}, bf16[128,2048]{1,0:T(8,128)(2,1)S(1)}, u32[]{:S(2)}, u32[]{:S(2)}) collective-permute-start(bf16[128,2048]{1,0:T(8,128)(2,1)} %get-tuple-element.11), channel_id=1, source_target_pairs={{0,2},{1,3},{2,0},{3,1},{4,6},{5,7},{6,4},{7,5},{8,10},{9,11},{10,... | collective-permute-start | bytes 1572872 | tf_op jit(solution)/shard_map/ppermute | solution.py:39
  281.2 8.7 %copy-start.10 = (u32[32]{0:T(128)S(1)}, u32[32]{0:T(128)}, u32[]{:S(2)}) copy-start(u32[32]{0:T(128)} %constant.25) | copy-start | bytes 388
  281.2 9.9 %copy-start.9 = (f32[1,2048]{1,0:T(1,128)S(1)}, f32[1,2048]{1,0:T(1,128)}, u32[]{:S(2)}) copy-start(f32[1,2048]{1,0:T(1,128)} %get-tuple-element.13) | copy-start | bytes 24580
  281.2 35.5 %collective-permute-start.4 = (bf16[256,3072]{1,0:T(8,128)(2,1)}, bf16[256,3072]{1,0:T(8,128)(2,1)S(1)}, u32[]{:S(2)}, u32[]{:S(2)}) collective-permute-start(bf16[256,3072]{1,0:T(8,128)(2,1)} %pad_maximum_fusion), channel_id=1, source_target_pairs={{0,1},{1,0},{2,3},{3,2},{4,5},{5,4},{6,7},{7,6},{8,9},{9,8},{10,11... | collective-permute-start | bytes 4718600 | tf_op jit(solution)/shard_map/ppermute | solution.py:39
  284.4 1.1 copy-start.3
  285.5 23.9 %collective-permute-start.6 = (bf16[256,2048]{1,0:T(8,128)(2,1)}, bf16[256,2048]{1,0:T(8,128)(2,1)}, u32[]{:S(2)}, u32[]{:S(2)}) collective-permute-start(bf16[256,2048]{1,0:T(8,128)(2,1)} %pad_maximum_fusion.2), channel_id=1, source_target_pairs={{0,1},{1,0},{2,3},{3,2},{4,5},{5,4},{6,7},{7,6},{8,9},{9,8},{10,11... | collective-permute-start | bytes 3145736 | tf_op jit(solution)/shard_map/ppermute | solution.py:39
  285.6 21.5 %copy-start = (bf16[128,3072]{1,0:T(8,128)(2,1)S(1)}, bf16[128,3072]{1,0:T(8,128)(2,1)}, u32[]{:S(2)}) copy-start(bf16[128,3072]{1,0:T(8,128)(2,1)} %get-tuple-element.10) | copy-start | bytes 2359300
  287.7 19.5 %collective-permute-start.9 = (bf16[128,1024]{1,0:T(8,128)(2,1)}, bf16[128,1024]{1,0:T(8,128)(2,1)}, u32[]{:S(2)}, u32[]{:S(2)}) collective-permute-start(bf16[128,1024]{1,0:T(8,128)(2,1)} %get-tuple-element.23), channel_id=1, source_target_pairs={{0,3},{1,2},{2,1},{3,0},{4,7},{5,6},{6,5},{7,4},{8,11},{9,10},{10,... | collective-permute-start | bytes 786440 | tf_op jit(solution)/shard_map/ppermute | solution.py:39
  289.4 18.0 %collective-permute-start.8 = (bf16[128,1024]{1,0:T(8,128)(2,1)}, bf16[128,1024]{1,0:T(8,128)(2,1)}, u32[]{:S(2)}, u32[]{:S(2)}) collective-permute-start(bf16[128,1024]{1,0:T(8,128)(2,1)} %get-tuple-element.24), channel_id=1, source_target_pairs={{0,1},{1,0},{2,3},{3,2},{4,5},{5,4},{6,7},{7,6},{8,9},{9,8},{10,11... | collective-permute-start | bytes 786440 | tf_op jit(solution)/shard_map/ppermute | solution.py:39
  289.4 18.6 %collective-permute-start.7 = (bf16[128,1024]{1,0:T(8,128)(2,1)}, bf16[128,1024]{1,0:T(8,128)(2,1)}, u32[]{:S(2)}, u32[]{:S(2)}) collective-permute-start(bf16[128,1024]{1,0:T(8,128)(2,1)} %get-tuple-element.25), channel_id=1, source_target_pairs={{0,2},{1,3},{2,0},{3,1},{4,6},{5,7},{6,4},{7,5},{8,10},{9,11},{10,... | collective-permute-start | bytes 786440 | tf_op jit(solution)/shard_map/ppermute | solution.py:39
  307.1 12.6 %copy-start.5 = (bf16[128,1024]{1,0:T(8,128)(2,1)}, bf16[128,1024]{1,0:T(8,128)(2,1)S(1)}, u32[]{:S(2)}) copy-start(bf16[128,1024]{1,0:T(8,128)(2,1)S(1)} %get-tuple-element.26) | copy-start | bytes 786436
  307.1 2.4 copy-start.2
  307.1 2.4 copy-start.4
  307.3 9.6 %collective-permute-start.2 = (bf16[128,1024]{1,0:T(8,128)(2,1)S(1)}, bf16[128,1024]{1,0:T(8,128)(2,1)S(1)}, u32[]{:S(2)}, u32[]{:S(2)}) collective-permute-start(bf16[128,1024]{1,0:T(8,128)(2,1)S(1)} %get-tuple-element.27), channel_id=1, source_target_pairs={{0,3},{1,2},{2,1},{3,0},{4,7},{5,6},{6,5},{7,4},{8,11},{9,10},{10,... | collective-permute-start | bytes 786440 | tf_op jit(solution)/shard_map/ppermute | solution.py:39
  307.3 9.5 %collective-permute-start.1 = (bf16[128,1024]{1,0:T(8,128)(2,1)S(1)}, bf16[128,1024]{1,0:T(8,128)(2,1)S(1)}, u32[]{:S(2)}, u32[]{:S(2)}) collective-permute-start(bf16[128,1024]{1,0:T(8,128)(2,1)S(1)} %get-tuple-element.28), channel_id=1, source_target_pairs={{0,1},{1,0},{2,3},{3,2},{4,5},{5,4},{6,7},{7,6},{8,9},{9,8},{10,11... | collective-permute-start | bytes 786440 | tf_op jit(solution)/shard_map/ppermute | solution.py:39
  308.0 11.7 %collective-permute-start = (bf16[128,1024]{1,0:T(8,128)(2,1)S(1)}, bf16[128,1024]{1,0:T(8,128)(2,1)S(1)}, u32[]{:S(2)}, u32[]{:S(2)}) collective-permute-start(bf16[128,1024]{1,0:T(8,128)(2,1)S(1)} %get-tuple-element.29), channel_id=1, source_target_pairs={{0,2},{1,3},{2,0},{3,1},{4,6},{5,7},{6,4},{7,5},{8,10},{9,11},{10,... | collective-permute-start | bytes 786440 | tf_op jit(solution)/shard_map/ppermute | solution.py:39
  316.8 6.2 %copy-start.7 = (bf16[512,3072]{1,0:T(8,128)(2,1)}, bf16[512,3072]{1,0:T(8,128)(2,1)S(1)}, u32[]{:S(2)}) copy-start(bf16[512,3072]{1,0:T(8,128)(2,1)S(1)} %constant_dynamic-update-slice_fusion) | copy-start | bytes 9437188
  323.0 5.3 %copy-start.6 = (bf16[128,1024]{1,0:T(8,128)(2,1)S(1)}, bf16[128,1024]{1,0:T(8,128)(2,1)}, u32[]{:S(2)}) copy-start(bf16[128,1024]{1,0:T(8,128)(2,1)} %copy-done.5) | copy-start | bytes 786436

commit v3 on v2

v3 whole, which is shorter than its diff:
```python
import functools

import jax
import jax.numpy as jnp
from jax import lax
from jax.experimental import pallas as pl
from jax.experimental.pallas import tpu as pltpu
from jax.sharding import PartitionSpec as P

HEAD_DIM = 128


EPS = 1e-05
NEG = -1e30


def inner(former, latter):
    return lax.dot_general(
        former, latter, (((0,), (0,)), ((), ())), preferred_element_type=jnp.float32
    )


def outer_side(former, latter):
    return lax.dot_general(
        former, latter, (((1,), (1,)), ((), ())), preferred_element_type=jnp.float32
    )


def plain(former, latter):
    return jnp.dot(former, latter, preferred_element_type=jnp.float32)


def row_dot(former, latter):
    return jnp.sum(former.astype(jnp.float32) * latter.astype(jnp.float32), -1, keepdims=True)


def tile_of(width):
    return 512 if width % 512 == 0 else 256


def tiles(width, body):
    size = tile_of(width)

    def step(index, carry):
        body(pl.multiple_of(index * size, size), size)
        return carry

    lax.fori_loop(0, width // size, step, 0)


def kernel(
    ranks, sections, replicas, micro,
    hidden, mask, gains, wq_hbm, wkv_hbm, wo_hbm, grad_out,
    normed_all, mixed_all, pair_all, grad_all, gain_sum,
    normed, grad_rows, gain_grad,
    wq, wkv, wo, hfull, gfull, gain_all, scales, queries, keyval, weights, mix_grad,
    send_f, recv_f, send_b, recv_b, next_h, next_g, corr_out, corr_in,
    load_sem, gain_sem, ag_sem, rs_sem, z_sem, corr_sem, cut_sem, line_sem, core_sem, sum_sem,
):
    rank = lax.axis_index("tensor")
    station = lax.axis_index("section")
    rows = hidden.shape[1]
    width = hidden.shape[2]
    model = ranks * width
    q_width = wq.shape[1]
    pairs = wkv.shape[1] // (2 * HEAD_DIM)
    group = q_width // (HEAD_DIM * pairs)
    chunk = tile_of(width)
    chunks = width // chunk
    mixed, pair_rows = mixed_all.at[0], pair_all.at[0]
    replica = lax.axis_index("dp")
    lines = replicas // 2
    slots = [(d, c) for c in (0, 1) for d in range(lines)]
    cut = model // replicas
    first, last = station == 0, station == sections - 1

    def peer(distance):
        return lax.rem(rank + distance, ranks)

    def twin(slot):
        line = lax.rem(lax.div(replica, 2) + slot[0], lines)
        core = lax.rem(replica + slot[1], 2)
        return line * 2 + core

    def remote(source, target, sems, device):
        return pltpu.make_async_remote_copy(
            src_ref=source, dst_ref=target, send_sem=sems[0], recv_sem=sems[1],
            device_id=device, device_id_type=pl.DeviceIdType.MESH,
        )

    barrier = pltpu.get_barrier_semaphore()
    for distance in range(1, ranks):
        pl.semaphore_signal(
            barrier, inc=1, device_id={"tensor": peer(distance)},
            device_id_type=pl.DeviceIdType.MESH,
        )

    for slot in slots[1:]:
        pl.semaphore_signal(
            barrier, inc=1, device_id={"dp": twin(slot)},
            device_id_type=pl.DeviceIdType.MESH,
        )

    @pl.when(station > 0)
    def _():
        pl.semaphore_signal(
            barrier, inc=1, device_id={"section": station - 1},
            device_id_type=pl.DeviceIdType.MESH,
        )

    @pl.when(station < sections - 1)
    def _():
        pl.semaphore_signal(
            barrier, inc=1, device_id={"section": station + 1},
            device_id_type=pl.DeviceIdType.MESH,
        )

    loads = [
        pltpu.make_async_copy(source, target, load_sem.at[index])
        for index, (source, target) in enumerate(((wq_hbm, wq), (wkv_hbm, wkv), (wo_hbm, wo)))
    ]

    def source_copy(way, m):
        return pltpu.make_async_copy(
            (hidden, grad_out)[way].at[m], (hfull, gfull)[way].at[m, rank],
            load_sem.at[3 + way * micro + m],
        )

    @pl.when(first)
    def _():
        for m in range(micro):
            source_copy(0, m).start()

    @pl.when(last)
    def _():
        for m in range(micro):
            source_copy(1, m).start()

    for load in loads:
        load.start()

    ends = jnp.where(first, 0, 1) + jnp.where(last, 0, 1)
    pl.semaphore_wait(barrier, ranks - 1 + replicas - 1 + ends)

    def gain_copy(distance):
        return remote(
            gain_all.at[rank], gain_all.at[rank],
            (gain_sem.at[0, distance - 1], gain_sem.at[1, distance - 1]),
            {"tensor": peer(distance)},
        )

    def columns_of(index):
        return pl.ds(pl.multiple_of(index * chunk, chunk), chunk)

    def gather_copy(way, m, index, distance):
        block = (hfull, gfull)[way].at[m, rank, :, columns_of(index)]
        return remote(
            block, block,
            (ag_sem.at[way, 0, m, index, distance - 1], ag_sem.at[way, 1, m, index, distance - 1]),
            {"tensor": peer(distance)},
        )

    def sum_copy(way, m, index, distance):
        columns = columns_of(index)
        return remote(
            (send_f, send_b)[way].at[m, distance - 1, :, columns],
            (recv_f, recv_b)[way].at[m, distance - 1, :, columns],
            (rs_sem.at[way, 0, m, index, distance - 1], rs_sem.at[way, 1, m, index, distance - 1]),
            {"tensor": peer(distance)},
        )

    def corr_copy(m, distance):
        return remote(
            corr_out.at[m], corr_in.at[m, distance - 1],
            (corr_sem.at[0, m, distance - 1], corr_sem.at[1, m, distance - 1]),
            {"tensor": peer(distance)},
        )

    def hop_copy(way, m, index):
        target = station + 1 if way == 0 else station - 1
        target = lax.rem(target + sections, sections)
        columns = columns_of(index)
        return remote(
            (next_h, next_g)[way].at[m, :, columns],
            (hfull, gfull)[way].at[m, rank, :, columns],
            (z_sem.at[way, 0, m, index], z_sem.at[way, 1, m, index]),
            {"section": target},
        )

    def spread(way, m, index):
        for distance in range(1, ranks):
            gather_copy(way, m, index, distance).start()

    def line_of(m):
        return pl.ds(pl.multiple_of(m * rows, rows), rows)

    def cut_copy(kind, m, place):
        target = twin(slots[place])
        source = (normed, grad_rows)[kind]
        return remote(
            source.at[line_of(m), pl.ds(pl.multiple_of(target * cut, cut), cut)],
            (normed_all, grad_all)[kind].at[place, line_of(m)],
            (cut_sem.at[kind, 0, m, place - 1], cut_sem.at[kind, 1, m, place - 1]),
            {"dp": target},
        )

    def start_cut(kind, m):
        own_cut = pl.ds(pl.multiple_of(replica * cut, cut), cut)
        (normed_all, grad_all)[kind][0, line_of(m)] = (normed, grad_rows)[kind][line_of(m), own_cut]
        for place in range(1, replicas):
            cut_copy(kind, m, place).start()

    def line_copy(kind, m, place):
        whole = (mixed_all, pair_all)[kind]
        return remote(
            whole.at[0, line_of(m)], whole.at[place, line_of(m)],
            (line_sem.at[kind, 0, m, place - 1], line_sem.at[kind, 1, m, place - 1]),
            {"dp": twin((place, 0))},
        )

    def core_copy(kind, m, place):
        whole = (mixed_all, pair_all)[kind]
        return remote(
            whole.at[place, line_of(m)], whole.at[lines + place, line_of(m)],
            (core_sem.at[kind, 0, m, place], core_sem.at[kind, 1, m, place]),
            {"dp": twin((0, 1))},
        )

    def start_rows(kind, m):
        for place in range(1, lines):
            line_copy(kind, m, place).start()
        core_copy(kind, m, 0).start()

    def pass_rows(kind, m):
        for place in range(1, lines):
            line_copy(kind, m, place).wait_recv()
            core_copy(kind, m, place).start()

    def total_copy(place):
        return remote(
            gain_grad.at[0], gain_grad.at[place],
            (sum_sem.at[0, place - 1], sum_sem.at[1, place - 1]),
            {"dp": twin(slots[place])},
        )

    gain_all[rank] = gains[...]
    for distance in range(1, ranks):
        gain_copy(distance).start()

    @pl.when(first)
    def _():
        for m in range(micro):
            source_copy(0, m).wait()
            for index in range(chunks):
                spread(0, m, index)

    @pl.when(last)
    def _():
        for m in range(micro):
            source_copy(1, m).wait()
            for index in range(chunks):
                spread(1, m, index)

    for distance in range(1, ranks):
        gain_copy(distance).wait()

    def gather(way, m, at_source):
        @pl.when(jnp.logical_not(at_source))
        def _():
            for index in range(chunks):
                hop_copy(way, m, index).wait_recv()
                spread(way, m, index)

        for index in range(chunks):
            for distance in range(1, ranks):
                gather_copy(way, m, index, distance).wait()

    def gain_of(owner):
        return gain_all[owner][:1].astype(jnp.float32)

    def stack(block):
        return jnp.concatenate(
            [block[:, a * HEAD_DIM:(a + 1) * HEAD_DIM] for a in range(group)], 0
        )

    def head_parts(m, g):
        query = stack(queries[m, :, g * group * HEAD_DIM:(g + 1) * group * HEAD_DIM])
        key = keyval[m, :, 2 * g * HEAD_DIM:(2 * g + 1) * HEAD_DIM]
        value = keyval[m, :, (2 * g + 1) * HEAD_DIM:(2 * g + 2) * HEAD_DIM]
        return query, key, value

    def forward(m, carry):
        gather(0, m, first)
        line = line_of(m)
        total = jnp.zeros((rows, 1), jnp.float32)
        for owner in range(ranks):
            wide = hfull[m, owner].astype(jnp.float32)
            total = total + jnp.sum(wide * wide, -1, keepdims=True)
        scale = lax.rsqrt(total / model + EPS)
        scales[m] = jnp.broadcast_to(scale, (rows, HEAD_DIM))
        for owner in range(ranks):
            wide = hfull[m, owner].astype(jnp.float32)
            normed[line, owner * width:(owner + 1) * width] = (
                wide * scale * gain_of(owner)
            ).astype(jnp.bfloat16)

        start_cut(0, m)

        @pl.when(m == 0)
        def _():
            loads[0].wait()
            loads[1].wait()

        def project_q(start, size):
            columns = pl.ds(start, size)
            queries[m, :, columns] = plain(normed[line, :], wq[:, columns]).astype(jnp.bfloat16)

        def project_kv(start, size):
            columns = pl.ds(start, size)
            keyval[m, :, columns] = plain(normed[line, :], wkv[:, columns]).astype(jnp.bfloat16)

        tiles(q_width, project_q)
        tiles(wkv.shape[1], project_kv)
        allowed = jnp.concatenate([mask[m]] * group, 0) > 0.5
        for g in range(pairs):
            query, key, value = head_parts(m, g)
            scores = outer_side(query, key) * HEAD_DIM ** (-0.5)
            scores = jnp.where(allowed, scores, NEG)
            raised = jnp.exp(scores - jnp.max(scores, -1, keepdims=True))
            attn = raised / jnp.sum(raised, -1, keepdims=True)
            weights[m, g] = attn
            mix = plain(attn.astype(jnp.bfloat16), value).astype(jnp.bfloat16)
            for a in range(group):
                at = (g * group + a) * HEAD_DIM
                mixed[line, at:at + HEAD_DIM] = mix[a * rows:(a + 1) * rows]

        start_rows(0, m)

        @pl.when(m == 0)
        def _():
            loads[2].wait()

        @pl.when(jnp.logical_not(last))
        def _():
            for distance in range(1, ranks):
                base = peer(distance) * width

                def project_far(start, size):
                    far = pl.ds(pl.multiple_of(base + start, size), size)
                    send_f[m, distance - 1, :, pl.ds(start, size)] = plain(
                        mixed[line, :], wo[:, far]
                    ).astype(jnp.bfloat16)
                    sum_copy(0, m, lax.div(start, size), distance).start()

                tiles(width, project_far)

            def project_own(start, size):
                near = pl.ds(pl.multiple_of(rank * width + start, size), size)
                index, columns = lax.div(start, size), pl.ds(start, size)
                result = plain(mixed[line, :], wo[:, near])
                for distance in range(1, ranks):
                    sum_copy(0, m, index, distance).wait()
                    result = result + recv_f[m, distance - 1, :, columns].astype(jnp.float32)
                next_h[m, :, columns] = (
                    hfull[m, rank, :, columns].astype(jnp.float32) + result
                ).astype(jnp.bfloat16)
                hop_copy(0, m, index).start()

            tiles(width, project_own)

        return carry

    lax.fori_loop(0, micro, forward, 0)
    gain_grad[0] = jnp.zeros(gain_grad.shape[1:], jnp.float32)

    def backward(m, carry):
        gather(1, m, last)
        line = line_of(m)
        for owner in range(ranks):
            grad_rows[line, owner * width:(owner + 1) * width] = gfull[m, owner]
        start_cut(1, m)

        def back_out(start, size):
            part = pl.ds(start, size)
            mix_grad[:, part] = outer_side(grad_rows[line, :], wo[part, :]).astype(jnp.bfloat16)

        tiles(q_width, back_out)
        correction = jnp.zeros((rows, 1), jnp.float32)
        for g in range(pairs):
            query, key, value = head_parts(m, g)
            attn = weights[m, g]
            grads = stack(mix_grad[:, g * group * HEAD_DIM:(g + 1) * group * HEAD_DIM])
            value_grad = inner(attn.astype(jnp.bfloat16), grads).astype(jnp.bfloat16)
            weight_grad = outer_side(grads, value)
            score_grad = (
                attn
                * (weight_grad - jnp.sum(weight_grad * attn, -1, keepdims=True))
                * HEAD_DIM ** (-0.5)
            ).astype(jnp.bfloat16)
            query_grad = plain(score_grad, key).astype(jnp.bfloat16)
            key_grad = inner(score_grad, query).astype(jnp.bfloat16)
            query_part = row_dot(query_grad, query)
            correction = correction + row_dot(key_grad, key) + row_dot(value_grad, value)
            for a in range(group):
                correction = correction + query_part[a * rows:(a + 1) * rows]
                at = (g * group + a) * HEAD_DIM
                pair_rows[line, at:at + HEAD_DIM] = query_grad[a * rows:(a + 1) * rows]
            at = q_width + 2 * g * HEAD_DIM
            pair_rows[line, at:at + HEAD_DIM] = key_grad
            pair_rows[line, at + HEAD_DIM:at + 2 * HEAD_DIM] = value_grad

        def back_in(base, start, size):
            part = pl.ds(pl.multiple_of(base + start, size), size)
            return outer_side(pair_rows[line, :q_width], wq[part, :]) + outer_side(
                pair_rows[line, q_width:], wkv[part, :]
            )

        scale = scales[m][:, :1]
        corr_out[m] = jnp.broadcast_to(correction / scale, (rows, HEAD_DIM))
        for distance in range(1, ranks):
            corr_copy(m, distance).start()
        start_rows(1, m)

        for distance in range(1, ranks):
            owner = peer(distance)

            def far(start, size):
                partial = back_in(owner * width, start, size)
                send_b[m, distance - 1, :, pl.ds(start, size)] = partial.astype(jnp.bfloat16)
                sum_copy(1, m, lax.div(start, size), distance).start()

            tiles(width, far)

        total = corr_out[m]
        for distance in range(1, ranks):
            corr_copy(m, distance).wait()
            total = total + corr_in[m, distance - 1]
        factor = scale * scale * scale / model * total[:, :1]

        def near(start, size):
            index, columns = lax.div(start, size), pl.ds(start, size)
            partial = back_in(rank * width, start, size)
            for distance in range(1, ranks):
                sum_copy(1, m, index, distance).wait()
                partial = partial + recv_b[m, distance - 1, :, columns].astype(jnp.float32)
            wide = hfull[m, rank, :, columns].astype(jnp.float32)
            gain = gain_all[rank, :, columns][:1].astype(jnp.float32)

            @pl.when(station > 0)
            def _():
                next_g[m, :, columns] = (
                    gfull[m, rank, :, columns].astype(jnp.float32)
                    + scale * gain * partial
                    - wide * factor
                ).astype(jnp.bfloat16)
                hop_copy(1, m, index).start()

            gain_grad[0, :, columns] += jnp.broadcast_to(
                jnp.sum(partial * wide * scale, 0, keepdims=True), (8, size)
            )

        tiles(width, near)
        pass_rows(0, m)
        pass_rows(1, m)
        return carry

    lax.fori_loop(0, micro, backward, 0)
    for place in range(1, replicas):
        total_copy(place).start()
    for m in range(micro):
        for kind in range(2):
            for place in range(1, replicas):
                cut_copy(kind, m, place).wait()
            for place in range(1, lines):
                line_copy(kind, m, place).wait_send()
            for place in range(lines):
                core_copy(kind, m, place).wait()
    total = gain_grad[0]
    for place in range(1, replicas):
        total_copy(place).wait()
        total = total + gain_grad[place]
    gain_sum[...] = total

    @pl.when(jnp.logical_not(last))
    def _():
        for m in range(micro):
            for index in range(chunks):
                hop_copy(0, m, index).wait_send()

    @pl.when(station > 0)
    def _():
        for m in range(micro):
            for index in range(chunks):
                hop_copy(1, m, index).wait_send()


def layers(hidden_in, mask, gains, query_weight, pair_weight, out_weight, grad_out):
    ranks, sections = lax.axis_size("tensor"), lax.axis_size("section")
    replicas = lax.axis_size("dp")
    micro, rows, width = hidden_in.shape
    model = ranks * width
    q_width, kv_width = query_weight.shape[1], pair_weight.shape[1]
    pairs = kv_width // (2 * HEAD_DIM)
    group = q_width // (HEAD_DIM * pairs)
    half, wide = jnp.bfloat16, jnp.float32
    vmem = pl.BlockSpec(memory_space=pltpu.VMEM)
    anywhere = pl.BlockSpec(memory_space=pl.ANY)
    others, lines, chunks = ranks - 1, replicas // 2, width // tile_of(width)
    return pl.pallas_call(
        functools.partial(kernel, ranks, sections, replicas, micro),
        out_shape=(
            jax.ShapeDtypeStruct((replicas, micro * rows, model // replicas), half),
            jax.ShapeDtypeStruct((replicas, micro * rows, q_width), half),
            jax.ShapeDtypeStruct((replicas, micro * rows, q_width + kv_width), half),
            jax.ShapeDtypeStruct((replicas, micro * rows, model // replicas), half),
            jax.ShapeDtypeStruct((8, width), wide),
        ),
        in_specs=[anywhere, vmem, vmem, anywhere, anywhere, anywhere, anywhere],
        out_specs=(vmem,) * 5,
        scratch_shapes=[
            pltpu.VMEM((micro * rows, model), half),
            pltpu.VMEM((micro * rows, model), half),
            pltpu.VMEM((replicas, 8, width), wide),
            pltpu.VMEM((model, q_width), half),
            pltpu.VMEM((model, kv_width), half),
            pltpu.VMEM((q_width, model), half),
            pltpu.VMEM((micro, ranks, rows, width), half),
            pltpu.VMEM((micro, ranks, rows, width), half),
            pltpu.VMEM((ranks, 16, width), half),
            pltpu.VMEM((micro, rows, HEAD_DIM), wide),
            pltpu.VMEM((micro, rows, q_width), half),
            pltpu.VMEM((micro, rows, kv_width), half),
            pltpu.VMEM((micro, pairs, group * rows, rows), wide),
            pltpu.VMEM((rows, q_width), half),
            pltpu.VMEM((micro, others, rows, width), half),
            pltpu.VMEM((micro, others, rows, width), half),
            pltpu.VMEM((micro, others, rows, width), half),
            pltpu.VMEM((micro, others, rows, width), half),
            pltpu.VMEM((micro, rows, width), half),
            pltpu.VMEM((micro, rows, width), half),
            pltpu.VMEM((micro, rows, HEAD_DIM), wide),
            pltpu.VMEM((micro, others, rows, HEAD_DIM), wide),
            pltpu.SemaphoreType.DMA((3 + 2 * micro,)),
            pltpu.SemaphoreType.DMA((2, others)),
            pltpu.SemaphoreType.DMA((2, 2, micro, chunks, others)),
            pltpu.SemaphoreType.DMA((2, 2, micro, chunks, others)),
            pltpu.SemaphoreType.DMA((2, 2, micro, chunks)),
            pltpu.SemaphoreType.DMA((2, micro, others)),
            pltpu.SemaphoreType.DMA((2, 2, micro, replicas - 1)),
            pltpu.SemaphoreType.DMA((2, 2, micro, max(lines - 1, 1))),
            pltpu.SemaphoreType.DMA((2, 2, micro, lines)),
            pltpu.SemaphoreType.DMA((2, replicas - 1)),
        ],
        compiler_params=pltpu.CompilerParams(
            collective_id=0, has_side_effects=True, vmem_limit_bytes=60 << 20
        ),
    )(hidden_in, mask, gains, query_weight, pair_weight, out_weight, grad_out)


def shards(hidden_in, lengths, gains, w_query, w_keyval, w_out, grad_out):
    row_count = hidden_in.shape[1]
    query_weight = w_query[0]
    model_width = query_weight.shape[0]
    pair_count = w_keyval.shape[2]
    pair_weight = w_keyval[0].reshape(model_width, -1)
    position = jnp.arange(row_count)
    causal = position[None, :] <= position[:, None]
    mask = (causal[None] & (position[None, None, :] < lengths[:, None, None])).astype(jnp.float32)
    gain_rows = jnp.broadcast_to(gains, (16, gains.shape[1]))
    *gathered, gain_sum = layers(
        hidden_in, mask, gain_rows, query_weight, pair_weight, w_out[0], grad_out
    )
    normed_rows, mixed_rows, pair_rows, outgrad_rows = [
        block.reshape(-1, block.shape[2]) for block in gathered
    ]
    query_width = query_weight.shape[1]
    query_total = inner(normed_rows, pair_rows[:, :query_width])
    pair_total = inner(normed_rows, pair_rows[:, query_width:])
    output_total = inner(mixed_rows, outgrad_rows)
    gain_width = gain_sum.shape[1] // lax.axis_size("dp")
    gain_total = lax.dynamic_slice_in_dim(gain_sum[0], lax.axis_index("dp") * gain_width, gain_width)
    grad_query = query_total[None]
    grad_keyval = pair_total.reshape(1, pair_total.shape[0], pair_count, 2 * HEAD_DIM)
    grad_outproj = output_total[None]
    grad_gain = gain_total[None]
    return (grad_query, grad_keyval, grad_outproj, grad_gain)


def solution(mesh):
    in_specs = (
        P("dp", None, "tensor"),
        P("dp"),
        P("section", "tensor"),
        P("section", None, "tensor"),
        P("section", None, "tensor", None),
        P("section", "tensor", None),
        P("dp", None, "tensor"),
    )
    out_specs = (
        P("section", "dp", "tensor"),
        P("section", "dp", "tensor", None),
        P("section", "tensor", "dp"),
        P("section", ("tensor", "dp")),
    )
    return jax.shard_map(shards, mesh=mesh, in_specs=in_specs, out_specs=out_specs, check_vma=False)
```

time: 336 us -> 251 us (0.75)
  Pallas kernels: 254 us -> 217 us
  waiting for transfers between devices: 16.3 us -> 0 us
  blocking collectives: 14 us -> 0 us
  starting transfers between devices: 6.43 us -> 0 us
  matrix products: 17.9 us -> 12.9 us
    pallas_call x1, Pallas kernels: 254 us -> 217 us  [layers(): pl.pallas_call(functools.partial(kernel, ranks, sections, replicas, micro...]
    ppermute x10 -> x0, waiting for transfers between devices: 16.3 us -> none  [exchange(): lax.ppermute(block, 'dp', [(i, i ^ mask) for i in range(lax.axis_size('dp...]
    unnamed x1 -> x0, blocking collectives: 14 us -> none
    ppermute x10 -> x0, starting transfers between devices: 6.43 us -> none  [exchange(): lax.ppermute(block, 'dp', [(i, i ^ mask) for i in range(lax.axis_size('dp...]
    dot_general x3, matrix products: 17.9 us -> 12.9 us  [inner(): lax.dot_general(former, latter, (((0,), (0,)), ((), ())), preferred_eleme...]
    concatenate x2 -> x0, other arithmetic: 3.47 us -> none  [every_row(): block = jnp.concatenate([block, exchange(block, bit)], 0)]
    unnamed x28 -> x10, local copies, waits for them, and re-layouts: 16.2 us -> 14.3 us
  transfers between devices with their start and end apart: 10 -> 0, of which waited for: 3 -> 0; matrix products, arithmetic and copies ran while one was open for 5% -> 0% of each run, Pallas kernels for 0% -> 0%
where the time goes in v3:
time: 251 us
  Pallas kernels  217 us (86%)
  local copies, waits for them, and re-layouts  18.4 us (7%)
  matrix products  12.9 us (5%)
    pallas_call x1, Pallas kernels, layers(): pl.pallas_call(functools.partial(kernel, ranks, sections, replicas, micro...  217 us
    unnamed x10, local copies, waits for them, and re-layouts  14.3 us
    dot_general x3, matrix products, inner(): lax.dot_general(former, latter, (((0,), (0,)), ((), ())), preferred_eleme...  12.9 us

profile of v3, /device:TPU:0, one launch (start us, length us, event | category | flops | bytes accessed | tf_op | source)
XLA Modules:
  0.0 251.0 jit_solution(8460238643156179846)
XLA Ops:
  0.6 0.7 iota_compare_fusion.1
  1.4 0.7 reduce
  2.1 0.6 and_convert_fusion.mask
  2.7 0.6 broadcast_in_dim.9.gains
  3.4 9.5 %copy.18 = bf16[512,8,4,256]{3,1,2,0:T(8,128)(2,1)} copy(bf16[512,8,4,256]{3,2,1,0:T(4,128)(2,1)} %bitcast.27) | data formatting | bytes 16777216
  12.9 216.9 %shard_map.102 = (bf16[4,128,1024]{2,1,0:T(8,128)(2,1)}, bf16[4,128,2048]{2,1,0:T(8,128)(2,1)}, bf16[4,128,3072]{2,1,0:T(8,128)(2,1)}, bf16[4,128,1024]{2,1,0:T(8,128)(2,1)}, f32[8,2048]{1,0:T(8,128)}) custom-call(bf16[2,64,2048]{2,1,0:T(8,128)(2,1)} %hidden.1, f32[2,64,64]{2,1,0:T(8,128)} %and_convert_fusion.mask, bf16[16,2048]{1,0:T(8,128)(2,1)} %broadcast_in_dim.9.gains, ...), custom_call_target="tpu_custom_call" | custom-call | tf_op jit(solution)/shard_map/pallas_call | solution.py:509
  229.8 0.0 copy-start.3
  229.8 0.9 slice.11
  230.7 0.6 constant_dynamic-slice_fusion
  231.3 1.3 slice_bitcast_fusion
  232.6 0.7 copy.11
  233.3 0.0 copy-done.3
  233.3 1.3 convolution_bitcast_fusion.2
  234.6 0.0 copy-start
  234.6 4.7 %copy.14 = f32[1,1024,4,256]{3,2,1,0:T(4,128)} copy(f32[1,1024,4,256]{3,1,2,0:T(8,128)S(1)} %convolution_bitcast_fusion.2) | data formatting | bytes 8388608
  239.4 0.0 copy-done
  239.4 0.0 copy-start.1
  239.4 0.0 copy-start.2
  239.4 5.8 %convolution_bitcast_fusion.1 = f32[1,1024,2048]{2,1,0:T(8,128)} fusion(bf16[512,1024]{1,0:T(8,128)(2,1)S(1)} %bitcast.32, bf16[512,3072]{1,0:T(8,128)(2,1)S(1)} %bitcast.30), kind=kOutput, calls=%fused_computation.1 | convolution fusion | flops 2147483648 | bytes 11534336 | tf_op jit(solution)/shard_map/dot_general | solution.py:18
  245.2 0.0 copy-done.1
  245.2 0.0 copy-done.2
  245.2 5.8 %convolution_bitcast_fusion = f32[1,2048,1024]{2,1,0:T(8,128)} fusion(bf16[4,128,2048]{2,1,0:T(8,128)(2,1)S(1)} %copy-done.1, bf16[4,128,1024]{2,1,0:T(8,128)(2,1)S(1)} %copy-done.2), kind=kOutput, calls=%fused_computation | convolution fusion | flops 2147483648 | bytes 11534336 | tf_op jit(solution)/shard_map/dot_general | solution.py:18
  (1 shorter events, 0.0 us)
Async XLA Ops:
  229.8 3.6 %copy-start.3 = (bf16[4,128,1024]{2,1,0:T(8,128)(2,1)S(1)}, bf16[4,128,1024]{2,1,0:T(8,128)(2,1)}, u32[]{:S(2)}) copy-start(bf16[4,128,1024]{2,1,0:T(8,128)(2,1)} %get-tuple-element.9) | copy-start | bytes 3145732
  234.6 4.7 %copy-start = (bf16[4,128,3072]{2,1,0:T(8,128)(2,1)S(1)}, bf16[4,128,3072]{2,1,0:T(8,128)(2,1)}, u32[]{:S(2)}) copy-start(bf16[4,128,3072]{2,1,0:T(8,128)(2,1)} %get-tuple-element.10) | copy-start | bytes 9437188
  239.4 5.8 %copy-start.1 = (bf16[4,128,2048]{2,1,0:T(8,128)(2,1)S(1)}, bf16[4,128,2048]{2,1,0:T(8,128)(2,1)}, u32[]{:S(2)}) copy-start(bf16[4,128,2048]{2,1,0:T(8,128)(2,1)} %get-tuple-element.11) | copy-start | bytes 6291460
  239.4 5.8 %copy-start.2 = (bf16[4,128,1024]{2,1,0:T(8,128)(2,1)S(1)}, bf16[4,128,1024]{2,1,0:T(8,128)(2,1)}, u32[]{:S(2)}) copy-start(bf16[4,128,1024]{2,1,0:T(8,128)(2,1)} %get-tuple-element.12) | copy-start | bytes 3145732

commit v4 on v3

--- a/solution.py
+++ b/solution.py
@@ -52,7 +52,7 @@
     ranks, sections, replicas, micro,
     hidden, mask, gains, wq_hbm, wkv_hbm, wo_hbm, grad_out,
     normed_all, mixed_all, pair_all, grad_all, gain_sum,
-    normed, grad_rows, gain_grad,
+    normed, gain_grad, acc,
     wq, wkv, wo, hfull, gfull, gain_all, scales, queries, keyval, weights, mix_grad,
     send_f, recv_f, send_b, recv_b, next_h, next_g, corr_out, corr_in,
     load_sem, gain_sem, ag_sem, rs_sem, z_sem, corr_sem, cut_sem, line_sem, core_sem, sum_sem,
@@ -194,19 +194,23 @@
     def line_of(m):
         return pl.ds(pl.multiple_of(m * rows, rows), rows)
 
+    def cut_of(kind, m, target):
+        if kind == 0:
+            return normed.at[line_of(m), pl.ds(pl.multiple_of(target * cut, cut), cut)]
+        start = lax.rem(target * cut, width)
+        return gfull.at[m, lax.div(target * cut, width), :, pl.ds(pl.multiple_of(start, cut), cut)]
+
     def cut_copy(kind, m, place):
         target = twin(slots[place])
-        source = (normed, grad_rows)[kind]
-        return remote(
-            source.at[line_of(m), pl.ds(pl.multiple_of(target * cut, cut), cut)],
+        return remote(
+            cut_of(kind, m, target),
             (normed_all, grad_all)[kind].at[place, line_of(m)],
             (cut_sem.at[kind, 0, m, place - 1], cut_sem.at[kind, 1, m, place - 1]),
             {"dp": target},
         )
 
     def start_cut(kind, m):
-        own_cut = pl.ds(pl.multiple_of(replica * cut, cut), cut)
-        (normed_all, grad_all)[kind][0, line_of(m)] = (normed, grad_rows)[kind][line_of(m), own_cut]
+        (normed_all, grad_all)[kind][0, line_of(m)] = cut_of(kind, m, replica)[...]
         for place in range(1, replicas):
             cut_copy(kind, m, place).start()
 
@@ -264,16 +268,30 @@
     for distance in range(1, ranks):
         gain_copy(distance).wait()
 
-    def gather(way, m, at_source):
-        @pl.when(jnp.logical_not(at_source))
-        def _():
-            for index in range(chunks):
+    def gather(way, m, at_source, use):
+        def near(index, carry):
+            @pl.when(jnp.logical_not(at_source))
+            def _():
                 hop_copy(way, m, index).wait_recv()
                 spread(way, m, index)
 
-        for index in range(chunks):
-            for distance in range(1, ranks):
+            use(rank, columns_of(index), features_of(rank, index))
+            return carry
+
+        acc[...] = jnp.zeros(acc.shape, jnp.float32)
+        lax.fori_loop(0, chunks, near, 0)
+        for distance in range(1, ranks):
+            owner = lax.rem(rank - distance + ranks, ranks)
+
+            def far(index, carry, distance=distance, owner=owner):
                 gather_copy(way, m, index, distance).wait()
+                use(owner, columns_of(index), features_of(owner, index))
+                return carry
+
+            lax.fori_loop(0, chunks, far, 0)
+
+    def features_of(owner, index):
+        return pl.ds(pl.multiple_of(owner * width + index * chunk, chunk), chunk)
 
     def gain_of(owner):
         return gain_all[owner][:1].astype(jnp.float32)
@@ -290,37 +308,30 @@
         return query, key, value
 
     def forward(m, carry):
-        gather(0, m, first)
         line = line_of(m)
-        total = jnp.zeros((rows, 1), jnp.float32)
-        for owner in range(ranks):
-            wide = hfull[m, owner].astype(jnp.float32)
-            total = total + jnp.sum(wide * wide, -1, keepdims=True)
-        scale = lax.rsqrt(total / model + EPS)
-        scales[m] = jnp.broadcast_to(scale, (rows, HEAD_DIM))
-        for owner in range(ranks):
-            wide = hfull[m, owner].astype(jnp.float32)
-            normed[line, owner * width:(owner + 1) * width] = (
-                wide * scale * gain_of(owner)
-            ).astype(jnp.bfloat16)
-
-        start_cut(0, m)
 
         @pl.when(m == 0)
         def _():
             loads[0].wait()
             loads[1].wait()
 
-        def project_q(start, size):
-            columns = pl.ds(start, size)
-            queries[m, :, columns] = plain(normed[line, :], wq[:, columns]).astype(jnp.bfloat16)
-
-        def project_kv(start, size):
-            columns = pl.ds(start, size)
-            keyval[m, :, columns] = plain(normed[line, :], wkv[:, columns]).astype(jnp.bfloat16)
-
-        tiles(q_width, project_q)
-        tiles(wkv.shape[1], project_kv)
+        scales[m] = jnp.zeros((rows, HEAD_DIM), jnp.float32)
+
+        def project(owner, columns, part):
+            wide = hfull[m, owner, :, columns].astype(jnp.float32)
+            scales[m] += jnp.broadcast_to(
+                jnp.sum(wide * wide, -1, keepdims=True), (rows, HEAD_DIM)
+            )
+            gain = gain_all[owner, :, columns][:1].astype(jnp.float32)
+            raised = (wide * gain).astype(jnp.bfloat16)
+            acc[:, :q_width] += plain(raised, wq[part, :])
+            acc[:, q_width:] += plain(raised, wkv[part, :])
+
+        gather(0, m, first, project)
+        scale = lax.rsqrt(scales[m][:, :1] / model + EPS)
+        scales[m] = jnp.broadcast_to(scale, (rows, HEAD_DIM))
+        queries[m] = (acc[:, :q_width] * scale).astype(jnp.bfloat16)
+        keyval[m] = (acc[:, q_width:] * scale).astype(jnp.bfloat16)
         allowed = jnp.concatenate([mask[m]] * group, 0) > 0.5
         for g in range(pairs):
             query, key, value = head_parts(m, g)
@@ -368,23 +379,26 @@
 
             tiles(width, project_own)
 
+        for owner in range(ranks):
+            wide = hfull[m, owner].astype(jnp.float32)
+            normed[line, owner * width:(owner + 1) * width] = (
+                wide * scale * gain_of(owner)
+            ).astype(jnp.bfloat16)
+        start_cut(0, m)
         return carry
 
     lax.fori_loop(0, micro, forward, 0)
     gain_grad[0] = jnp.zeros(gain_grad.shape[1:], jnp.float32)
 
     def backward(m, carry):
-        gather(1, m, last)
         line = line_of(m)
-        for owner in range(ranks):
-            grad_rows[line, owner * width:(owner + 1) * width] = gfull[m, owner]
+
+        def back_out(owner, columns, part):
+            acc[:, :q_width] += outer_side(gfull[m, owner, :, columns], wo[:, part])
+
+        gather(1, m, last, back_out)
+        mix_grad[...] = acc[:, :q_width].astype(jnp.bfloat16)
         start_cut(1, m)
-
-        def back_out(start, size):
-            part = pl.ds(start, size)
-            mix_grad[:, part] = outer_side(grad_rows[line, :], wo[part, :]).astype(jnp.bfloat16)
-
-        tiles(q_width, back_out)
         correction = jnp.zeros((rows, 1), jnp.float32)
         for g in range(pairs):
             query, key, value = head_parts(m, g)
@@ -519,8 +533,8 @@
         out_specs=(vmem,) * 5,
         scratch_shapes=[
             pltpu.VMEM((micro * rows, model), half),
-            pltpu.VMEM((micro * rows, model), half),
             pltpu.VMEM((replicas, 8, width), wide),
+            pltpu.VMEM((rows, q_width + kv_width), wide),
             pltpu.VMEM((model, q_width), half),
             pltpu.VMEM((model, kv_width), half),
             pltpu.VMEM((q_width, model), half),

time: 251 us -> 217 us (0.86)
  Pallas kernels: 217 us -> 183 us
    pallas_call x1, Pallas kernels: 217 us -> 183 us  [layers(): pl.pallas_call(functools.partial(kernel, ranks, sections, replicas, micro...]
where the time goes in v4:
time: 217 us
  Pallas kernels  183 us (84%)
  local copies, waits for them, and re-layouts  18.4 us (8%)
  matrix products  12.9 us (6%)
    pallas_call x1, Pallas kernels, layers(): pl.pallas_call(functools.partial(kernel, ranks, sections, replicas, micro...  183 us
    unnamed x10, local copies, waits for them, and re-layouts  14.3 us
    dot_general x3, matrix products, inner(): lax.dot_general(former, latter, (((0,), (0,)), ((), ())), preferred_eleme...  12.9 us

profile of v4, /device:TPU:0, one launch (start us, length us, event | category | flops | bytes accessed | tf_op | source)
XLA Modules:
  0.0 216.7 jit_solution(6450463187270298835)
XLA Ops:
  0.6 0.7 iota_compare_fusion.1
  1.4 0.7 reduce
  2.1 0.6 and_convert_fusion.mask
  2.7 0.6 broadcast_in_dim.9.gains
  3.4 9.5 %copy.18 = bf16[512,8,4,256]{3,1,2,0:T(8,128)(2,1)} copy(bf16[512,8,4,256]{3,2,1,0:T(4,128)(2,1)} %bitcast.27) | data formatting | bytes 16777216
  12.9 182.6 %shard_map.102 = (bf16[4,128,1024]{2,1,0:T(8,128)(2,1)}, bf16[4,128,2048]{2,1,0:T(8,128)(2,1)}, bf16[4,128,3072]{2,1,0:T(8,128)(2,1)}, bf16[4,128,1024]{2,1,0:T(8,128)(2,1)}, f32[8,2048]{1,0:T(8,128)}) custom-call(bf16[2,64,2048]{2,1,0:T(8,128)(2,1)} %hidden.1, f32[2,64,64]{2,1,0:T(8,128)} %and_convert_fusion.mask, bf16[16,2048]{1,0:T(8,128)(2,1)} %broadcast_in_dim.9.gains, ...), custom_call_target="tpu_custom_call" | custom-call | tf_op jit(solution)/shard_map/pallas_call | solution.py:523
  195.5 0.0 copy-start.3
  195.5 0.9 slice.11
  196.4 0.6 constant_dynamic-slice_fusion
  197.0 1.3 slice_bitcast_fusion
  198.3 0.7 copy.11
  199.0 0.0 copy-done.3
  199.0 1.3 convolution_bitcast_fusion.2
  200.3 0.0 copy-start
  200.4 4.7 %copy.14 = f32[1,1024,4,256]{3,2,1,0:T(4,128)} copy(f32[1,1024,4,256]{3,1,2,0:T(8,128)S(1)} %convolution_bitcast_fusion.2) | data formatting | bytes 8388608
  205.1 0.0 copy-done
  205.1 0.0 copy-start.1
  205.1 0.0 copy-start.2
  205.1 5.8 %convolution_bitcast_fusion.1 = f32[1,1024,2048]{2,1,0:T(8,128)} fusion(bf16[512,1024]{1,0:T(8,128)(2,1)S(1)} %bitcast.32, bf16[512,3072]{1,0:T(8,128)(2,1)S(1)} %bitcast.30), kind=kOutput, calls=%fused_computation.1 | convolution fusion | flops 2147483648 | bytes 11534336 | tf_op jit(solution)/shard_map/dot_general | solution.py:18
  210.9 0.0 copy-done.1
  210.9 0.0 copy-done.2
  210.9 5.8 %convolution_bitcast_fusion = f32[1,2048,1024]{2,1,0:T(8,128)} fusion(bf16[4,128,2048]{2,1,0:T(8,128)(2,1)S(1)} %copy-done.1, bf16[4,128,1024]{2,1,0:T(8,128)(2,1)S(1)} %copy-done.2), kind=kOutput, calls=%fused_computation | convolution fusion | flops 2147483648 | bytes 11534336 | tf_op jit(solution)/shard_map/dot_general | solution.py:18
  (1 shorter events, 0.0 us)
Async XLA Ops:
  195.5 3.6 %copy-start.3 = (bf16[4,128,1024]{2,1,0:T(8,128)(2,1)S(1)}, bf16[4,128,1024]{2,1,0:T(8,128)(2,1)}, u32[]{:S(2)}) copy-start(bf16[4,128,1024]{2,1,0:T(8,128)(2,1)} %get-tuple-element.9) | copy-start | bytes 3145732
  200.3 4.7 %copy-start = (bf16[4,128,3072]{2,1,0:T(8,128)(2,1)S(1)}, bf16[4,128,3072]{2,1,0:T(8,128)(2,1)}, u32[]{:S(2)}) copy-start(bf16[4,128,3072]{2,1,0:T(8,128)(2,1)} %get-tuple-element.10) | copy-start | bytes 9437188
  205.1 5.8 %copy-start.1 = (bf16[4,128,2048]{2,1,0:T(8,128)(2,1)S(1)}, bf16[4,128,2048]{2,1,0:T(8,128)(2,1)}, u32[]{:S(2)}) copy-start(bf16[4,128,2048]{2,1,0:T(8,128)(2,1)} %get-tuple-element.11) | copy-start | bytes 6291460
  205.1 5.8 %copy-start.2 = (bf16[4,128,1024]{2,1,0:T(8,128)(2,1)S(1)}, bf16[4,128,1024]{2,1,0:T(8,128)(2,1)}, u32[]{:S(2)}) copy-start(bf16[4,128,1024]{2,1,0:T(8,128)(2,1)} %get-tuple-element.12) | copy-start | bytes 3145732

commit v5 on v4

--- a/solution.py
+++ b/solution.py
@@ -55,7 +55,7 @@
     normed, gain_grad, acc,
     wq, wkv, wo, hfull, gfull, gain_all, scales, queries, keyval, weights, mix_grad,
     send_f, recv_f, send_b, recv_b, next_h, next_g, corr_out, corr_in,
-    load_sem, gain_sem, ag_sem, rs_sem, z_sem, corr_sem, cut_sem, line_sem, core_sem, sum_sem,
+    load_sem, part_sem, gain_sem, ag_sem, rs_sem, z_sem, corr_sem, cut_sem, line_sem, core_sem, sum_sem,
 ):
     rank = lax.axis_index("tensor")
     station = lax.axis_index("section")
@@ -115,10 +115,17 @@
             device_id_type=pl.DeviceIdType.MESH,
         )
 
-    loads = [
-        pltpu.make_async_copy(source, target, load_sem.at[index])
-        for index, (source, target) in enumerate(((wq_hbm, wq), (wkv_hbm, wkv), (wo_hbm, wo)))
-    ]
+    def features_of(owner, index):
+        return pl.ds(pl.multiple_of(owner * width + index * chunk, chunk), chunk)
+
+    def weight_copies(owner, index):
+        part, place = features_of(owner, index), owner * chunks + index
+        return [
+            pltpu.make_async_copy(source.at[part], target.at[part], part_sem.at[kind, place])
+            for kind, (source, target) in enumerate(((wq_hbm, wq), (wkv_hbm, wkv)))
+        ]
+
+    out_load = pltpu.make_async_copy(wo_hbm, wo, load_sem.at[2])
 
     def source_copy(way, m):
         return pltpu.make_async_copy(
@@ -136,8 +143,11 @@
         for m in range(micro):
             source_copy(1, m).start()
 
-    for load in loads:
-        load.start()
+    for distance in range(ranks):
+        for index in range(chunks):
+            for load in weight_copies(lax.rem(rank - distance + ranks, ranks), index):
+                load.start()
+    out_load.start()
 
     ends = jnp.where(first, 0, 1) + jnp.where(last, 0, 1)
     pl.semaphore_wait(barrier, ranks - 1 + replicas - 1 + ends)
@@ -275,7 +285,7 @@
                 hop_copy(way, m, index).wait_recv()
                 spread(way, m, index)
 
-            use(rank, columns_of(index), features_of(rank, index))
+            use(rank, index)
             return carry
 
         acc[...] = jnp.zeros(acc.shape, jnp.float32)
@@ -285,13 +295,10 @@
 
             def far(index, carry, distance=distance, owner=owner):
                 gather_copy(way, m, index, distance).wait()
-                use(owner, columns_of(index), features_of(owner, index))
+                use(owner, index)
                 return carry
 
             lax.fori_loop(0, chunks, far, 0)
-
-    def features_of(owner, index):
-        return pl.ds(pl.multiple_of(owner * width + index * chunk, chunk), chunk)
 
     def gain_of(owner):
         return gain_all[owner][:1].astype(jnp.float32)
@@ -310,14 +317,15 @@
     def forward(m, carry):
         line = line_of(m)
 
-        @pl.when(m == 0)
-        def _():
-            loads[0].wait()
-            loads[1].wait()
-
         scales[m] = jnp.zeros((rows, HEAD_DIM), jnp.float32)
 
-        def project(owner, columns, part):
+        def project(owner, index):
+            @pl.when(m == 0)
+            def _():
+                for load in weight_copies(owner, index):
+                    load.wait()
+
+            columns, part = columns_of(index), features_of(owner, index)
             wide = hfull[m, owner, :, columns].astype(jnp.float32)
             scales[m] += jnp.broadcast_to(
                 jnp.sum(wide * wide, -1, keepdims=True), (rows, HEAD_DIM)
@@ -349,7 +357,7 @@
 
         @pl.when(m == 0)
         def _():
-            loads[2].wait()
+            out_load.wait()
 
         @pl.when(jnp.logical_not(last))
         def _():
@@ -393,7 +401,8 @@
     def backward(m, carry):
         line = line_of(m)
 
-        def back_out(owner, columns, part):
+        def back_out(owner, index):
+            columns, part = columns_of(index), features_of(owner, index)
             acc[:, :q_width] += outer_side(gfull[m, owner, :, columns], wo[:, part])
 
         gather(1, m, last, back_out)
@@ -555,6 +564,7 @@
             pltpu.VMEM((micro, rows, HEAD_DIM), wide),
             pltpu.VMEM((micro, others, rows, HEAD_DIM), wide),
             pltpu.SemaphoreType.DMA((3 + 2 * micro,)),
+            pltpu.SemaphoreType.DMA((2, ranks * chunks)),
             pltpu.SemaphoreType.DMA((2, others)),
             pltpu.SemaphoreType.DMA((2, 2, micro, chunks, others)),
             pltpu.SemaphoreType.DMA((2, 2, micro, chunks, others)),

time: 217 us -> 219 us (level)
    pallas_call x1, Pallas kernels: 183 us -> 185 us  [layers(): pl.pallas_call(functools.partial(kernel, ranks, sections, replicas, micro...]
where the time goes in v5:
time: 219 us
  Pallas kernels  185 us (84%)
  local copies, waits for them, and re-layouts  18.4 us (8%)
  matrix products  12.9 us (6%)
    pallas_call x1, Pallas kernels, layers(): pl.pallas_call(functools.partial(kernel, ranks, sections, replicas, micro...  185 us
    unnamed x10, local copies, waits for them, and re-layouts  14.3 us
    dot_general x3, matrix products, inner(): lax.dot_general(former, latter, (((0,), (0,)), ((), ())), preferred_eleme...  12.9 us

profile of v5, /device:TPU:0, one launch (start us, length us, event | category | flops | bytes accessed | tf_op | source)
XLA Modules:
  0.0 219.1 jit_solution(3130669540281037268)
XLA Ops:
  0.6 0.7 iota_compare_fusion.1
  1.4 0.7 reduce
  2.1 0.6 and_convert_fusion.mask
  2.7 0.6 broadcast_in_dim.9.gains
  3.4 9.5 %copy.18 = bf16[512,8,4,256]{3,1,2,0:T(8,128)(2,1)} copy(bf16[512,8,4,256]{3,2,1,0:T(4,128)(2,1)} %bitcast.27) | data formatting | bytes 16777216
  12.9 185.0 %shard_map.102 = (bf16[4,128,1024]{2,1,0:T(8,128)(2,1)}, bf16[4,128,2048]{2,1,0:T(8,128)(2,1)}, bf16[4,128,3072]{2,1,0:T(8,128)(2,1)}, bf16[4,128,1024]{2,1,0:T(8,128)(2,1)}, f32[8,2048]{1,0:T(8,128)}) custom-call(bf16[2,64,2048]{2,1,0:T(8,128)(2,1)} %hidden.1, f32[2,64,64]{2,1,0:T(8,128)} %and_convert_fusion.mask, bf16[16,2048]{1,0:T(8,128)(2,1)} %broadcast_in_dim.9.gains, ...), custom_call_target="tpu_custom_call" | custom-call | tf_op jit(solution)/shard_map/pallas_call | solution.py:532
  197.9 0.0 copy-start.3
  197.9 0.9 slice.11
  198.9 0.6 constant_dynamic-slice_fusion
  199.4 1.3 slice_bitcast_fusion
  200.7 0.7 copy.11
  201.5 0.0 copy-done.3
  201.5 1.3 convolution_bitcast_fusion.2
  202.8 0.0 copy-start
  202.8 4.7 %copy.14 = f32[1,1024,4,256]{3,2,1,0:T(4,128)} copy(f32[1,1024,4,256]{3,1,2,0:T(8,128)S(1)} %convolution_bitcast_fusion.2) | data formatting | bytes 8388608
  207.5 0.0 copy-done
  207.5 0.0 copy-start.1
  207.5 0.0 copy-start.2
  207.5 5.8 %convolution_bitcast_fusion.1 = f32[1,1024,2048]{2,1,0:T(8,128)} fusion(bf16[512,1024]{1,0:T(8,128)(2,1)S(1)} %bitcast.32, bf16[512,3072]{1,0:T(8,128)(2,1)S(1)} %bitcast.30), kind=kOutput, calls=%fused_computation.1 | convolution fusion | flops 2147483648 | bytes 11534336 | tf_op jit(solution)/shard_map/dot_general | solution.py:18
  213.3 0.0 copy-done.1
  213.3 0.0 copy-done.2
  213.3 5.8 %convolution_bitcast_fusion = f32[1,2048,1024]{2,1,0:T(8,128)} fusion(bf16[4,128,2048]{2,1,0:T(8,128)(2,1)S(1)} %copy-done.1, bf16[4,128,1024]{2,1,0:T(8,128)(2,1)S(1)} %copy-done.2), kind=kOutput, calls=%fused_computation | convolution fusion | flops 2147483648 | bytes 11534336 | tf_op jit(solution)/shard_map/dot_general | solution.py:18
  (1 shorter events, 0.0 us)
Async XLA Ops:
  197.9 3.6 %copy-start.3 = (bf16[4,128,1024]{2,1,0:T(8,128)(2,1)S(1)}, bf16[4,128,1024]{2,1,0:T(8,128)(2,1)}, u32[]{:S(2)}) copy-start(bf16[4,128,1024]{2,1,0:T(8,128)(2,1)} %get-tuple-element.9) | copy-start | bytes 3145732
  202.8 4.7 %copy-start = (bf16[4,128,3072]{2,1,0:T(8,128)(2,1)S(1)}, bf16[4,128,3072]{2,1,0:T(8,128)(2,1)}, u32[]{:S(2)}) copy-start(bf16[4,128,3072]{2,1,0:T(8,128)(2,1)} %get-tuple-element.10) | copy-start | bytes 9437188
  207.5 5.8 %copy-start.1 = (bf16[4,128,2048]{2,1,0:T(8,128)(2,1)S(1)}, bf16[4,128,2048]{2,1,0:T(8,128)(2,1)}, u32[]{:S(2)}) copy-start(bf16[4,128,2048]{2,1,0:T(8,128)(2,1)} %get-tuple-element.11) | copy-start | bytes 6291460
  207.5 5.8 %copy-start.2 = (bf16[4,128,1024]{2,1,0:T(8,128)(2,1)S(1)}, bf16[4,128,1024]{2,1,0:T(8,128)(2,1)}, u32[]{:S(2)}) copy-start(bf16[4,128,1024]{2,1,0:T(8,128)(2,1)} %get-tuple-element.12) | copy-start | bytes 3145732
